TPU v7x, 256 devices: a whole 4x4x8 slice. The times are simulated.
256 devices in a mesh: dp: 8 (over y, z_hi), seq: 32 (over x, z_lo, core).
Axes of the slice: x: 4, y: 4, z: 8 (z_hi: 2, z_lo: 4; z = z_hi * 4 + z_lo), core: 2. Of those that a mesh axis runs over, the one named last changes fastest.
Arguments:
- queries: bfloat16 [32768, 3072], P(('dp', 'seq')), parts along dimension 0, may hold values from -8 to 8
- key_states: bfloat16 [32768, 384], P(('dp', 'seq')), parts along dimension 0, may hold values from -8 to 8
- value_states: bfloat16 [32768, 384], P(('dp', 'seq')), parts along dimension 0, may hold values from -6 to 6
- outputs: bfloat16 [32768, 3072], P(('dp', 'seq')), parts along dimension 0, may hold values from -6 to 6
- out_grad: bfloat16 [32768, 3072], P(('dp', 'seq')), parts along dimension 0, may hold values from -6 to 6
- window_start: int32 [8], P('dp'), parts along dimension 0, may hold values from 0 to 126976
- head_group: int32 [32], replicated, may hold values from 0 to 3, as said below
Outputs:
- query_grad: bfloat16 [32768, 3072], P(('dp', 'seq')), parts along dimension 0
- key_grad: bfloat16 [32768, 384], P(('dp', 'seq')), parts along dimension 0
- value_grad: bfloat16 [32768, 384], P(('dp', 'seq')), parts along dimension 0
There are 8 independent parts, one for each index of `dp`. A program takes and returns all parts, laid end to end along the dimension named above; an argument that names none is the same for every part. Nothing has to cross between parts.
Inputs may be any that keep to these rules, and one draw needn't show every extreme that they name: `head_group`: each of the 4 groups is named by exactly 8 heads.
All inputs are finite; a program needn't handle non-finite values.
Results may differ from a plain program's by a relative error of at most 0.015.
Values may be sent and summed in bfloat16 or wider, within the bound.
A program may use at most 64 MiB of HBM per device.

v0:
```python
import jax
import jax.numpy as jnp
from jax import lax
from jax.sharding import PartitionSpec as P

HEAD_DIM = 96
ROT_DIM = 24


def rotate(field, positions, turn_sign):
    half_rot = ROT_DIM // 2
    frequency = 10000.0 ** (-2.0 * jnp.arange(half_rot, dtype=jnp.float32) / ROT_DIM)
    angles = positions[:, None] * frequency[None, :]
    cosine = jnp.cos(angles)[:, None, :]
    sine_part = turn_sign * jnp.sin(angles)[:, None, :]
    first_half = field[..., :half_rot]
    second = field[..., half_rot:ROT_DIM]
    return jnp.concatenate(
        [
            first_half * cosine - second * sine_part,
            second * cosine + first_half * sine_part,
            field[..., ROT_DIM:],
        ],
        axis=-1,
    )


def head_grads(query_head, key_head, value_head, out_head, grad_head, block_size):
    length = query_head.shape[0]
    head_width = query_head.shape[1]
    block_count = length // block_size
    score_scale = head_width ** (-0.5)
    row_delta = jnp.sum(grad_head.astype(jnp.float32) * out_head.astype(jnp.float32), axis=1)
    row_index = jnp.arange(block_size, dtype=jnp.int32)
    contract_last = (((1,), (1,)), ((), ()))
    contract_first = (((0,), (0,)), ((), ()))

    def outer(query_block, outer_state):
        key_acc, value_acc, query_acc = outer_state
        query_start = query_block * block_size
        query_rows = lax.dynamic_slice_in_dim(query_head, query_start, block_size, 0)
        grad_rows = lax.dynamic_slice_in_dim(grad_head, query_start, block_size, 0)
        delta_rows = lax.dynamic_slice_in_dim(row_delta, query_start, block_size, 0)

        def block_scores(key_block):
            key_start = key_block * block_size
            key_rows = lax.dynamic_slice_in_dim(key_head, key_start, block_size, 0)
            raw_scores = (
                lax.dot_general(
                    query_rows, key_rows, contract_last, preferred_element_type=jnp.float32
                )
                * score_scale
            )
            allowed = (key_start + row_index)[None, :] <= (query_start + row_index)[:, None]
            return (jnp.where(allowed, raw_scores, -jnp.inf), key_rows)

        def statistic(key_block, stat_state):
            row_max, row_sum = stat_state
            scores, key_rows = block_scores(key_block)
            new_max = jnp.maximum(row_max, jnp.max(scores, axis=1))
            row_sum = row_sum * jnp.exp(row_max - new_max) + jnp.sum(
                jnp.exp(scores - new_max[:, None]), axis=1
            )
            return (new_max, row_sum)

        start_state = (
            jnp.full((block_size,), -jnp.inf, jnp.float32),
            jnp.zeros((block_size,), jnp.float32),
        )
        row_max, row_sum = lax.fori_loop(0, query_block + 1, statistic, start_state)
        log_total = row_max + jnp.log(row_sum)

        def gradient(key_block, inner_state):
            key_sum, value_sum, query_rows_grad = inner_state
            key_start = key_block * block_size
            scores, key_rows = block_scores(key_block)
            value_rows = lax.dynamic_slice_in_dim(value_head, key_start, block_size, 0)
            weights = jnp.exp(scores - log_total[:, None])
            weights_half = weights.astype(jnp.bfloat16)
            value_part = lax.dot_general(
                weights_half, grad_rows, contract_first, preferred_element_type=jnp.float32
            )
            dweights = lax.dot_general(
                grad_rows, value_rows, contract_last, preferred_element_type=jnp.float32
            )
            dscores = (weights * (dweights - delta_rows[:, None])).astype(jnp.bfloat16)
            query_rows_grad = query_rows_grad + jnp.dot(
                dscores, key_rows, preferred_element_type=jnp.float32
            )
            key_part = lax.dot_general(
                dscores, query_rows, contract_first, preferred_element_type=jnp.float32
            )
            old_key = lax.dynamic_slice_in_dim(key_sum, key_start, block_size, 0)
            key_sum = lax.dynamic_update_slice_in_dim(key_sum, old_key + key_part, key_start, 0)
            old_value = lax.dynamic_slice_in_dim(value_sum, key_start, block_size, 0)
            value_sum = lax.dynamic_update_slice_in_dim(
                value_sum, old_value + value_part, key_start, 0
            )
            return (key_sum, value_sum, query_rows_grad)

        empty_rows = jnp.zeros((block_size, head_width), jnp.float32)
        key_acc, value_acc, query_rows_grad = lax.fori_loop(
            0, query_block + 1, gradient, (key_acc, value_acc, empty_rows)
        )
        query_acc = lax.dynamic_update_slice_in_dim(query_acc, query_rows_grad, query_start, 0)
        return (key_acc, value_acc, query_acc)

    zeros_full = jnp.zeros((length, head_width), jnp.float32)
    key_acc, value_acc, query_acc = lax.fori_loop(
        0, block_count, outer, (zeros_full, zeros_full, zeros_full)
    )
    return (query_acc * score_scale, key_acc * score_scale, value_acc)


def per_device(queries, key_states, value_states, outputs, out_grad, window_start, head_group):
    head_width = HEAD_DIM
    dev_count = lax.axis_size("seq")
    my_index = lax.axis_index("seq")
    rows_here = queries.shape[0]
    heads_total = queries.shape[1] // head_width
    groups_total = key_states.shape[1] // head_width
    heads_here = heads_total // dev_count
    length = rows_here * dev_count
    block_size = min(length, max(1024, length // 32))
    token_pos = (
        window_start[0] + my_index * rows_here + jnp.arange(rows_here, dtype=jnp.int32)
    ).astype(jnp.float32)
    query_rot = (
        rotate(
            queries.reshape(rows_here, heads_total, head_width).astype(jnp.float32), token_pos, 1.0
        )
        .astype(jnp.bfloat16)
        .reshape(rows_here, heads_total * head_width)
    )
    key_three = rotate(
        key_states.reshape(rows_here, groups_total, head_width).astype(jnp.float32), token_pos, 1.0
    ).astype(jnp.bfloat16)
    query_all, out_all, grad_all = (
        lax.all_to_all(query_rot, "seq", split_axis=1, concat_axis=0, tiled=True),
        lax.all_to_all(outputs, "seq", split_axis=1, concat_axis=0, tiled=True),
        lax.all_to_all(out_grad, "seq", split_axis=1, concat_axis=0, tiled=True),
    )
    key_whole, value_whole = (
        lax.all_gather(
            key_three.reshape(rows_here, groups_total * head_width), "seq", axis=0, tiled=True
        ),
        lax.all_gather(value_states, "seq", axis=0, tiled=True),
    )
    head_slot = 0
    group_id = head_group[my_index * heads_here + head_slot]
    key_list = [lax.dynamic_slice_in_dim(key_whole, group_id * head_width, head_width, 1)]
    value_list = [lax.dynamic_slice_in_dim(value_whole, group_id * head_width, head_width, 1)]
    head_slot = 0
    query_part, key_part, value_part = head_grads(
        query_all, key_list[head_slot], value_list[head_slot], out_all, grad_all, block_size
    )
    query_half = query_part.astype(jnp.bfloat16)
    query_back = lax.all_to_all(query_half, "seq", split_axis=0, concat_axis=1, tiled=True)
    key_heads = key_part.astype(jnp.bfloat16)
    value_heads = value_part.astype(jnp.bfloat16)
    key_back, value_back = (
        lax.all_to_all(key_heads, "seq", split_axis=0, concat_axis=1, tiled=True),
        lax.all_to_all(value_heads, "seq", split_axis=0, concat_axis=1, tiled=True),
    )
    member = (head_group[:, None] == jnp.arange(groups_total, dtype=jnp.int32)[None, :]).astype(
        jnp.bfloat16
    )
    key_sum = jnp.einsum(
        "shd,hg->sgd",
        key_back.reshape(rows_here, heads_total, head_width),
        member,
        preferred_element_type=jnp.float32,
    )
    value_sum = jnp.einsum(
        "shd,hg->sgd",
        value_back.reshape(rows_here, heads_total, head_width),
        member,
        preferred_element_type=jnp.float32,
    )
    key_grad = key_sum.astype(jnp.bfloat16).reshape(rows_here, groups_total * head_width)
    value_grad = value_sum.astype(jnp.bfloat16).reshape(rows_here, groups_total * head_width)
    return (query_back, key_grad, value_grad)


def solution(mesh):
    placed = (
        P(("dp", "seq"), None),
        P(("dp", "seq"), None),
        P(("dp", "seq"), None),
        P(("dp", "seq"), None),
        P(("dp", "seq"), None),
        P("dp"),
        P(),
    )
    return jax.shard_map(
        per_device,
        mesh=mesh,
        in_specs=placed,
        out_specs=(P(("dp", "seq"), None), P(("dp", "seq"), None), P(("dp", "seq"), None)),
        check_vma=False,
    )
```

profile of v0, /device:TPU:1, one launch (start us, length us, event | category | flops | bytes accessed | tf_op | source)
XLA Modules:
  0.0 360.6 jit_solution(4678197996528161287)
XLA Ops:
  13.4 10.2 %all-to-all-start = ((bf16[128,32,96]{0,2,1:T(8,128)(2,1)}), bf16[128,32,96]{0,2,1:T(8,128)(2,1)S(1)}, u32[]{:S(2)}, u32[]{:S(2)}) async-start(bf16[128,32,96]{0,2,1:T(8,128)(2,1)} %pad_maximum_fusion), calls=%async_computation | async-start | bytes 1572864 | tf_op jit(solution)/shard_map/all_to_all | solution.py:139
  24.7 24.2 %all-to-all-done = bf16[128,32,96]{0,2,1:T(8,128)(2,1)S(1)} async-done(((bf16[128,32,96]{0,2,1:T(8,128)(2,1)}), bf16[128,32,96]{0,2,1:T(8,128)(2,1)S(1)}, u32[]{:S(2)}, u32[]{:S(2)}) %all-to-all-start) | async-done | bytes 786464 | tf_op jit(solution)/shard_map/all_to_all | solution.py:139
  48.9 4.9 %all-to-all-start.1 = ((bf16[128,32,96]{0,2,1:T(8,128)(2,1)}), bf16[128,32,96]{0,2,1:T(8,128)(2,1)S(1)}, u32[]{:S(2)}, u32[]{:S(2)}) async-start(bf16[128,32,96]{0,2,1:T(8,128)(2,1)} %bitcast.7), calls=%async_computation.1 | async-start | bytes 1572864 | tf_op jit(solution)/shard_map/all_to_all | solution.py:141
  55.0 24.2 %all-to-all-done.1 = bf16[128,32,96]{0,2,1:T(8,128)(2,1)S(1)} async-done(((bf16[128,32,96]{0,2,1:T(8,128)(2,1)}), bf16[128,32,96]{0,2,1:T(8,128)(2,1)S(1)}, u32[]{:S(2)}, u32[]{:S(2)}) %all-to-all-start.1) | async-done | bytes 786464 | tf_op jit(solution)/shard_map/all_to_all | solution.py:141
  79.3 4.5 %all-to-all-start.2 = ((bf16[128,32,96]{0,2,1:T(8,128)(2,1)}), bf16[128,32,96]{0,2,1:T(8,128)(2,1)S(1)}, u32[]{:S(2)}, u32[]{:S(2)}) async-start(bf16[128,32,96]{0,2,1:T(8,128)(2,1)} %bitcast.10), calls=%async_computation.2 | async-start | bytes 1572864 | tf_op jit(solution)/shard_map/all_to_all | solution.py:140
  87.7 18.4 %all-to-all-done.2 = bf16[128,32,96]{0,2,1:T(8,128)(2,1)S(1)} async-done(((bf16[128,32,96]{0,2,1:T(8,128)(2,1)}), bf16[128,32,96]{0,2,1:T(8,128)(2,1)S(1)}, u32[]{:S(2)}, u32[]{:S(2)}) %all-to-all-start.2) | async-done | bytes 786464 | tf_op jit(solution)/shard_map/all_to_all | solution.py:140
  108.8 51.9 %all-gather.5.cloned.1.call-done = bf16[4096,384]{1,0:T(8,128)(2,1)} async-done(((bf16[128,384]{1,0:T(8,128)(2,1)}), bf16[4096,384]{1,0:T(8,128)(2,1)}) %all-gather.5.cloned.1.call-update) | async-done | bytes 3145744 | tf_op jit(solution)/shard_map/all_gather | solution.py:147
  166.4 103.5 %while.85 = (s32[]{:T(128)}, f32[4096,96]{0,1:T(8,128)S(1)}, f32[4096,96]{0,1:T(8,128)}, f32[4096,96]{0,1:T(8,128)}, bf16[4096,96]{1,0:T(8,128)(2,1)}, /*index=5...) while((s32[]{:T(128)}, f32[4096,96]{0,1:T(8,128)S(1)}, ...), condition=%wide.region_8.9_spmd.clone.clone, body=%wide.region_1.8_spmd.clone.clone.sunk | while | flops 1230281728 | bytes 33973152 | solution.py:109
  170.1 7.4 %while.87 = (s32[]{:T(128)}, f32[4096,96]{0,1:T(8,128)S(1)}, f32[4096,96]{0,1:T(8,128)}, f32[1024,96]{0,1:T(8,128)S(1)}, s32[]{:T(128)}, /*index=5*/s32[1024]{0:...) while((s32[]{:T(128)}, f32[4096,96]{0,1:T(8,128)S(1)}, ...), condition=%wide.region_7.7_spmd.clone, body=%wide.region_6.6_spmd.clone.sunk | while | flops 1019512832 | bytes 22978792 | solution.py:102
  180.1 3.7 %while.86 = (s32[]{:T(128)}, f32[1024]{0:T(1024)S(1)}, f32[1024]{0:T(1024)S(1)}, s32[]{:T(128)}, s32[1024]{0:T(1024)S(1)}, /*index=5*/s32[]{:T(128)}, bf16[4096,...) while((s32[]{:T(128)}, f32[1024]{0:T(1024)S(1)}, ...), condition=%wide.region_5.5_spmd.clone, body=%wide.region_2.4_spmd.clone.sunk | while | flops 210767872 | bytes 8994991 | solution.py:70
  183.9 14.9 %while.87 = (s32[]{:T(128)}, f32[4096,96]{0,1:T(8,128)S(1)}, f32[4096,96]{0,1:T(8,128)}, f32[1024,96]{0,1:T(8,128)S(1)}, s32[]{:T(128)}, /*index=5*/s32[1024]{0:...) while((s32[]{:T(128)}, f32[4096,96]{0,1:T(8,128)S(1)}, ...), condition=%wide.region_7.7_spmd.clone, body=%wide.region_6.6_spmd.clone.sunk | while | flops 1019512832 | bytes 22978792 | solution.py:102
  192.1 3.0 fusion.82
  201.4 5.6 %while.86 = (s32[]{:T(128)}, f32[1024]{0:T(1024)S(1)}, f32[1024]{0:T(1024)S(1)}, s32[]{:T(128)}, s32[1024]{0:T(1024)S(1)}, /*index=5*/s32[]{:T(128)}, bf16[4096,...) while((s32[]{:T(128)}, f32[1024]{0:T(1024)S(1)}, ...), condition=%wide.region_5.5_spmd.clone, body=%wide.region_2.4_spmd.clone.sunk | while | flops 210767872 | bytes 8994991 | solution.py:70
  207.0 22.3 %while.87 = (s32[]{:T(128)}, f32[4096,96]{0,1:T(8,128)S(1)}, f32[4096,96]{0,1:T(8,128)}, f32[1024,96]{0,1:T(8,128)S(1)}, s32[]{:T(128)}, /*index=5*/s32[1024]{0:...) while((s32[]{:T(128)}, f32[4096,96]{0,1:T(8,128)S(1)}, ...), condition=%wide.region_7.7_spmd.clone, body=%wide.region_6.6_spmd.clone.sunk | while | flops 1019512832 | bytes 22978792 | solution.py:102
  215.2 3.0 fusion.82
  231.9 7.4 %while.86 = (s32[]{:T(128)}, f32[1024]{0:T(1024)S(1)}, f32[1024]{0:T(1024)S(1)}, s32[]{:T(128)}, s32[1024]{0:T(1024)S(1)}, /*index=5*/s32[]{:T(128)}, bf16[4096,...) while((s32[]{:T(128)}, f32[1024]{0:T(1024)S(1)}, ...), condition=%wide.region_5.5_spmd.clone, body=%wide.region_2.4_spmd.clone.sunk | while | flops 210767872 | bytes 8994991 | solution.py:70
  239.3 29.7 %while.87 = (s32[]{:T(128)}, f32[4096,96]{0,1:T(8,128)S(1)}, f32[4096,96]{0,1:T(8,128)}, f32[1024,96]{0,1:T(8,128)S(1)}, s32[]{:T(128)}, /*index=5*/s32[1024]{0:...) while((s32[]{:T(128)}, f32[4096,96]{0,1:T(8,128)S(1)}, ...), condition=%wide.region_7.7_spmd.clone, body=%wide.region_6.6_spmd.clone.sunk | while | flops 1019512832 | bytes 22978792 | solution.py:102
  247.5 3.0 fusion.82
  272.3 5.4 %all-to-all-start.3 = ((bf16[32,128,96]{1,2,0:T(8,128)(2,1)}), bf16[32,128,96]{1,2,0:T(8,128)(2,1)}, u32[]{:S(2)}, u32[]{:S(2)}) async-start(bf16[32,128,96]{1,2,0:T(8,128)(2,1)} %copy_bitcast_fusion.2), calls=%async_computation.3 | async-start | bytes 1572864 | tf_op jit(solution)/shard_map/all_to_all | solution.py:158
  278.8 21.3 %all-to-all-done.3 = bf16[32,128,96]{1,2,0:T(8,128)(2,1)} async-done(((bf16[32,128,96]{1,2,0:T(8,128)(2,1)}), bf16[32,128,96]{1,2,0:T(8,128)(2,1)}, u32[]{:S(2)}, u32[]{:S(2)}) %all-to-all-start.3) | async-done | bytes 786464 | tf_op jit(solution)/shard_map/all_to_all | solution.py:158
  300.1 3.8 %all-to-all-start.4 = ((bf16[32,128,96]{1,2,0:T(8,128)(2,1)}), bf16[32,128,96]{1,2,0:T(8,128)(2,1)S(1)}, u32[]{:S(2)}, u32[]{:S(2)}) async-start(bf16[32,128,96]{1,2,0:T(8,128)(2,1)} %copy_bitcast_fusion.1), calls=%async_computation.4 | async-start | bytes 1572864 | tf_op jit(solution)/shard_map/all_to_all | solution.py:162
  304.9 21.4 %all-to-all-done.4 = bf16[32,128,96]{1,2,0:T(8,128)(2,1)S(1)} async-done(((bf16[32,128,96]{1,2,0:T(8,128)(2,1)}), bf16[32,128,96]{1,2,0:T(8,128)(2,1)S(1)}, u32[]{:S(2)}, u32[]{:S(2)}) %all-to-all-start.4) | async-done | bytes 786464 | tf_op jit(solution)/shard_map/all_to_all | solution.py:162
  326.4 3.8 %all-to-all-start.5 = ((bf16[32,128,96]{1,2,0:T(8,128)(2,1)}), bf16[32,128,96]{1,2,0:T(8,128)(2,1)S(1)}, u32[]{:S(2)}, u32[]{:S(2)}) async-start(bf16[32,128,96]{1,2,0:T(8,128)(2,1)} %copy_bitcast_fusion), calls=%async_computation.5 | async-start | bytes 1572864 | tf_op jit(solution)/shard_map/all_to_all | solution.py:163
  333.6 19.1 %all-to-all-done.5 = bf16[32,128,96]{1,2,0:T(8,128)(2,1)S(1)} async-done(((bf16[32,128,96]{1,2,0:T(8,128)(2,1)}), bf16[32,128,96]{1,2,0:T(8,128)(2,1)S(1)}, u32[]{:S(2)}, u32[]{:S(2)}) %all-to-all-start.5) | async-done | bytes 786464 | tf_op jit(solution)/shard_map/all_to_all | solution.py:163
  (200 shorter events, 123.1 us)
Async XLA Ops:
  7.2 99.8 %all-gather.3.cloned.1.call-start = ((), (), s32[]{:S(2)}) async-start(), calls=%async_computation.6 | async-start | bytes 3244032 | tf_op jit(solution)/shard_map/all_gather | solution.py:144
  9.8 150.9 %all-gather.5.cloned.1.call-start = ((), (), s32[]{:S(2)}) async-start(), calls=%async_computation.7 | async-start | bytes 3244032 | tf_op jit(solution)/shard_map/all_gather | solution.py:147
  12.3 11.3 %copy-start.1 = (bf16[128,3072]{1,0:T(8,128)(2,1)S(1)}, bf16[128,3072]{1,0:T(8,128)(2,1)}, u32[]{:S(2)}) copy-start(bf16[128,3072]{1,0:T(8,128)(2,1)} %param.17) | copy-start | bytes 2359300
  13.4 40.5 %copy-start.2 = (bf16[128,3072]{1,0:T(8,128)(2,1)S(1)}, bf16[128,3072]{1,0:T(8,128)(2,1)}, u32[]{:S(2)}) copy-start(bf16[128,3072]{1,0:T(8,128)(2,1)} %param.16) | copy-start | bytes 2359300
  13.4 35.6 %all-to-all-start = ((bf16[128,32,96]{0,2,1:T(8,128)(2,1)}), bf16[128,32,96]{0,2,1:T(8,128)(2,1)S(1)}, u32[]{:S(2)}, u32[]{:S(2)}) async-start(bf16[128,32,96]{0,2,1:T(8,128)(2,1)} %pad_maximum_fusion), calls=%async_computation | async-start | bytes 1572864 | tf_op jit(solution)/shard_map/all_to_all | solution.py:139
  48.9 34.9 %copy-start.3 = (s32[32]{0:T(128)S(1)}, s32[32]{0:T(128)}, u32[]{:S(2)}) copy-start(s32[32]{0:T(128)} %param.19) | copy-start | bytes 388
  48.9 30.3 %all-to-all-start.1 = ((bf16[128,32,96]{0,2,1:T(8,128)(2,1)}), bf16[128,32,96]{0,2,1:T(8,128)(2,1)S(1)}, u32[]{:S(2)}, u32[]{:S(2)}) async-start(bf16[128,32,96]{0,2,1:T(8,128)(2,1)} %bitcast.7), calls=%async_computation.1 | async-start | bytes 1572864 | tf_op jit(solution)/shard_map/all_to_all | solution.py:141
  79.3 26.9 %all-to-all-start.2 = ((bf16[128,32,96]{0,2,1:T(8,128)(2,1)}), bf16[128,32,96]{0,2,1:T(8,128)(2,1)S(1)}, u32[]{:S(2)}, u32[]{:S(2)}) async-start(bf16[128,32,96]{0,2,1:T(8,128)(2,1)} %bitcast.10), calls=%async_computation.2 | async-start | bytes 1572864 | tf_op jit(solution)/shard_map/all_to_all | solution.py:140
  272.3 27.8 %all-to-all-start.3 = ((bf16[32,128,96]{1,2,0:T(8,128)(2,1)}), bf16[32,128,96]{1,2,0:T(8,128)(2,1)}, u32[]{:S(2)}, u32[]{:S(2)}) async-start(bf16[32,128,96]{1,2,0:T(8,128)(2,1)} %copy_bitcast_fusion.2), calls=%async_computation.3 | async-start | bytes 1572864 | tf_op jit(solution)/shard_map/all_to_all | solution.py:158
  277.7 26.2 %copy-start = (f32[4096,96]{0,1:T(8,128)S(1)}, f32[4096,96]{0,1:T(8,128)}, u32[]{:S(2)}) copy-start(f32[4096,96]{0,1:T(8,128)} %get-tuple-element.309) | copy-start | bytes 4718596
  300.1 26.3 %all-to-all-start.4 = ((bf16[32,128,96]{1,2,0:T(8,128)(2,1)}), bf16[32,128,96]{1,2,0:T(8,128)(2,1)S(1)}, u32[]{:S(2)}, u32[]{:S(2)}) async-start(bf16[32,128,96]{1,2,0:T(8,128)(2,1)} %copy_bitcast_fusion.1), calls=%async_computation.4 | async-start | bytes 1572864 | tf_op jit(solution)/shard_map/all_to_all | solution.py:162
  304.9 27.5 %copy-start.4 = (s32[32]{0:T(128)S(1)}, s32[32]{0:T(128)}, u32[]{:S(2)}) copy-start(s32[32]{0:T(128)} %param.19) | copy-start | bytes 388
  326.4 26.3 %all-to-all-start.5 = ((bf16[32,128,96]{1,2,0:T(8,128)(2,1)}), bf16[32,128,96]{1,2,0:T(8,128)(2,1)S(1)}, u32[]{:S(2)}, u32[]{:S(2)}) async-start(bf16[32,128,96]{1,2,0:T(8,128)(2,1)} %copy_bitcast_fusion), calls=%async_computation.5 | async-start | bytes 1572864 | tf_op jit(solution)/shard_map/all_to_all | solution.py:163
Sparse Core Ops, SparseCore 0:
  10.3 86.4 all-gather.2
  98.7 61.9 all-gather.4
where the time goes:
time: 362 us; the launch traced here: 361 us
  waiting for transfers between devices  181 us (50%)
  matrix products  81.7 us (23%)
  starting transfers between devices  32.7 us (9%)
  local copies, waits for them, and re-layouts  29.9 us (8%)
  other arithmetic  17.9 us (5%)
  between operations  15.6 us (4%)
    all_gather x1, waiting for transfers between devices, per_device(): lax.all_gather(value_states, 'seq', axis=0, tiled=True)  51.9 us
    dot_general x10, matrix products, gradient(): lax.dot_general(weights_half, grad_rows, contract_first, preferred_elemen...  30.1 us
    all_to_all x1, waiting for transfers between devices, per_device(): lax.all_to_all(out_grad, 'seq', split_axis=1, concat_axis=0, tiled=True)  24.2 us
    all_to_all x1, waiting for transfers between devices, per_device(): lax.all_to_all(query_rot, 'seq', split_axis=1, concat_axis=0, tiled=True)  24.2 us
    dot_general x10, matrix products, gradient(): lax.dot_general(grad_rows, value_rows, contract_last, preferred_element_t...  23.1 us
    all_to_all x1, waiting for transfers between devices, per_device(): lax.all_to_all(key_heads, 'seq', split_axis=0, concat_axis=1, tiled=True)  21.4 us
    all_to_all x1, waiting for transfers between devices, per_device(): lax.all_to_all(query_half, 'seq', split_axis=0, concat_axis=1, tiled=True)  21.3 us
    all_to_all x1, waiting for transfers between devices, per_device(): lax.all_to_all(value_heads, 'seq', split_axis=0, concat_axis=1, tiled=True)  19.1 us
  transfers between devices with their start and end apart: 8, of which 7 were waited for; matrix products, arithmetic and copies ran while one was open for 5% of the time, Pallas kernels for 0%

commit v1 on v0

v1 whole, which is shorter than its diff:
```python
import functools
import math

import jax
import jax.numpy as jnp
from jax import lax
from jax.experimental import pallas as pl
from jax.experimental.pallas import tpu as pltpu
from jax.sharding import PartitionSpec as P

HEADS = 32
GROUPS = 4
WIDTH = 96
ROT_DIM = 24
F32 = jnp.float32
BF16 = jnp.bfloat16
LN2 = math.log(2.0)
SCALE = WIDTH**-0.5
NT = (((1,), (1,)), ((), ()))
VM = pltpu.VMEM
SIDE_ROWS = 784


def find_slots(group_ref, slot_ref, count_ref):
    for g in range(GROUPS):
        count_ref[g] = 0
    for h in range(HEADS):
        g = group_ref[h]
        rank = count_ref[g]
        slot_ref[h] = g * 8 + rank
        count_ref[g] = rank + 1


def split3(value):
    high = value.astype(BF16)
    rest = value - high.astype(F32)
    middle = rest.astype(BF16)
    low = (rest - middle.astype(F32)).astype(BF16)
    return high.astype(F32), middle.astype(F32), low.astype(F32)


def prep_kernel(group_ref, q_ref, k_ref, v_ref, o_ref, g_ref, turn_ref, side_ref, kv_ref,
                qt, ot, gt, kt, vt, delta, slot_ref, count_ref):
    find_slots(group_ref, slot_ref, count_ref)

    def flip(j, _):
        lanes = pl.ds(pl.multiple_of(j * 128, 128), 128)
        qt[lanes, :] = q_ref[:, lanes].T
        ot[lanes, :] = o_ref[:, lanes].T
        gt[lanes, :] = g_ref[:, lanes].T
        return 0

    lax.fori_loop(0, 24, flip, 0)
    for j in range(3):
        lanes = slice(j * 128, j * 128 + 128)
        kt[lanes, :] = k_ref[:, lanes].T
        vt[lanes, :] = v_ref[:, lanes].T
    cosine = turn_ref[0]
    sine = turn_ref[1]

    def turned(x):
        head = x[0:ROT_DIM]
        swapped = jnp.concatenate([x[12:24], x[0:12]], axis=0)
        return jnp.concatenate([head * cosine + swapped * sine, x[ROT_DIM:]], axis=0)

    def one_head(h, _):
        rows = pl.ds(pl.multiple_of(h * WIDTH, 32), WIDTH)
        slot = slot_ref[h]
        owner = slot // 4
        place = pl.multiple_of((slot % 4) * WIDTH, 32)
        x = turned(qt[rows, :].astype(F32)) * (SCALE / LN2)
        side_ref[owner, pl.ds(place, WIDTH), :] = x.astype(BF16)
        grad = gt[rows, :]
        side_ref[owner, pl.ds(place + 384, WIDTH), :] = grad
        delta[pl.ds(slot, 1), :] = jnp.sum(
            grad.astype(F32) * ot[rows, :].astype(F32), axis=0, keepdims=True
        )
        return 0

    lax.fori_loop(0, HEADS, one_head, 0)
    for owner in range(8):
        high, middle, low = split3(delta[owner * 4 : owner * 4 + 4, :])
        side_ref[owner, 768:784, :] = jnp.concatenate(
            [high, middle, low, jnp.zeros((4, 128), F32)], axis=0
        ).astype(BF16)
    for g in range(GROUPS):
        rows = slice(g * WIDTH, (g + 1) * WIDTH)
        kv_ref[g, 0:96, :] = turned(kt[rows, :].astype(F32)).astype(BF16)
        kv_ref[g, 96:192, :] = vt[rows, :]


def main_kernel(side_src, kv_src, dq_out, dkv_out,
                side, kv, S, Pm, QT, DO, Kn, Vn, KT, dKa, dVa, DQ,
                dq_src, part, core_in, total_r, total_l, final,
                s_side, r_side, s_kx, r_kx, s_kr, r_kr, s_kl, r_kl, s_kc, r_kc,
                s_dq, r_dq, s_pc, r_pc, s_tr, r_tr, s_tl, r_tl, s_f, r_f):
    me = lax.axis_index("seq")
    x = me // 8
    z = (me // 2) % 4
    c = me % 2
    mine = x * 2 + c

    def at(px, pz, pc):
        return {"seq": px * 8 + pz * 2 + pc}

    def remote(src, dst, send, recv, where):
        return pltpu.make_async_remote_copy(
            src_ref=src, dst_ref=dst, send_sem=send, recv_sem=recv,
            device_id=where, device_id_type=pl.DeviceIdType.MESH,
        )

    peers = [lax.rem(mine + j, 8) for j in range(1, 8)]
    barrier = pltpu.get_barrier_semaphore()
    for p in peers:
        pl.semaphore_signal(barrier, inc=1, device_id=at(p // 2, z, p % 2),
                            device_id_type=pl.DeviceIdType.MESH)

    @pl.when(z > 0)
    def _():
        pl.semaphore_signal(barrier, inc=1, device_id=at(x, z - 1, c),
                            device_id_type=pl.DeviceIdType.MESH)

    @pl.when(z < 3)
    def _():
        pl.semaphore_signal(barrier, inc=1, device_id=at(x, z + 1, c),
                            device_id_type=pl.DeviceIdType.MESH)

    pl.semaphore_wait(barrier, 7 + jnp.minimum(z, 1) + jnp.minimum(3 - z, 1))

    kx = []
    for j in range(1, 4):
        px = lax.rem(x + j, 4)
        copy = remote(kv_src.at[px], kv.at[z, c, x], s_kx.at[j], r_kx.at[x], at(px, z, c))
        copy.start()
        kx.append(copy)
    kv[z, c, x] = kv_src[x]
    moved = []
    for p in peers:
        copy = remote(side_src.at[p], side.at[mine], s_side.at[p], r_side.at[mine], at(p // 2, z, p % 2))
        copy.start()
        moved.append(copy)
    side[mine] = side_src[mine]
    for j in range(1, 4):
        px = lax.rem(x + j, 4)
        remote(kv_src.at[px], kv.at[z, c, px], s_kx.at[j], r_kx.at[px], at(px, z, c)).wait_recv()

    def to_core(b):
        return remote(kv.at[b, c], kv.at[b, c], s_kc.at[b], r_kc.at[b], at(x, z, 1 - c))

    def to_right(b):
        return remote(kv.at[b, c], kv.at[b, c], s_kr.at[b], r_kr.at[b], at(x, z + 1, c))

    def to_left(b):
        return remote(kv.at[b, c], kv.at[b, c], s_kl.at[b], r_kl.at[b], at(x, z - 1, c))

    @pl.when(z < 3)
    def _():
        to_right(z).start()

    @pl.when(z > 0)
    def _():
        to_left(z).start()

    to_core(z).start()
    for step in range(1, 4):
        low = z - step

        @pl.when(low >= 0)
        def _():
            to_right(low).wait_recv()

            @pl.when(z < 3)
            def _():
                to_right(low).start()

            to_core(low).start()

        high = z + step

        @pl.when(high <= 3)
        def _():
            to_left(high).wait_recv()

            @pl.when(z > 0)
            def _():
                to_left(high).start()

            to_core(high).start()

    for b in range(4):
        remote(kv.at[b, c], kv.at[b, 1 - c], s_kc.at[b], r_kc.at[b], at(x, z, 1 - c)).wait_recv()
        to_core(b).wait_send()

        @pl.when((b <= z) & (z < 3))
        def _():
            to_right(b).wait_send()

        @pl.when((b >= z) & (z > 0))
        def _():
            to_left(b).wait_send()

    for copy in kx:
        copy.wait_send()
    for p, copy in zip(peers, moved):
        remote(side_src.at[p], side.at[p], s_side.at[p], r_side.at[p], at(p // 2, z, p % 2)).wait_recv()
        copy.wait_send()

    one_rows = (lax.broadcasted_iota(jnp.int32, (32, 128), 0) < 3).astype(BF16)
    zero_rows = jnp.zeros((32, 128), BF16)
    for half in range(2):
        lanes = slice(half * 128, half * 128 + 128)

        def stage(i, _):
            b = i // 4
            px = i % 4
            block = kv[b, half, px]
            keys = block[0:96]
            KT[px * 4 + b, :, lanes] = keys
            Kn[px * 4 + b, lanes, :] = jnp.concatenate([keys, zero_rows], 0).T
            Vn[px * 4 + b, lanes, :] = jnp.concatenate([block[96:192], one_rows], 0).T
            return 0

        lax.fori_loop(0, 16, stage, 0)

    def clear(i, _):
        dKa[i] = jnp.zeros((96, 256), F32)
        dVa[i] = jnp.zeros((96, 256), F32)
        return 0

    lax.fori_loop(0, 16, clear, 0)
    allowed = lax.broadcasted_iota(jnp.int32, (256, 256), 0) <= lax.broadcasted_iota(
        jnp.int32, (256, 256), 1
    )
    row_id = lax.broadcasted_iota(jnp.int32, (32, 128), 0)
    QT[96:128, :] = jnp.zeros((32, 1024), BF16)

    def query_block(qx, _):
        for h in range(4):
            for half in range(2):
                start = h * 256 + half * 128
                QT[0:96, start : start + 128] = side[qx * 2 + half, h * 96 : h * 96 + 96, :]
        count = qx * 4 + z + 1

        def scores(kb, state):
            result = []
            for h in range(4):
                lanes = slice(h * 256, h * 256 + 256)
                s = jnp.dot(Kn[kb], QT[:, lanes], preferred_element_type=F32)
                S[kb, :, lanes] = s
                result.append(jnp.maximum(state[h], jnp.max(s.reshape(32, 8, 256), axis=0)))
            return tuple(result)

        state = tuple(jnp.full((8, 256), -1e30, F32) for _ in range(4))
        state = lax.fori_loop(0, count - 1, scores, state)
        top = []
        for h in range(4):
            lanes = slice(h * 256, h * 256 + 256)
            s = jnp.dot(Kn[count - 1], QT[:, lanes], preferred_element_type=F32)
            s = jnp.where(allowed, s, -1e30)
            S[count - 1, :, lanes] = s
            high = jnp.maximum(state[h], jnp.max(s.reshape(32, 8, 256), axis=0))
            top.append(jnp.max(high, axis=0, keepdims=True))

        def weigh(kb, sums):
            result = []
            for h in range(4):
                lanes = slice(h * 256, h * 256 + 256)
                p = jnp.exp2(S[kb, :, lanes] - top[h])
                Pm[kb, :, lanes] = p.astype(BF16)
                result.append(sums[h] + jnp.sum(p.reshape(32, 8, 256), axis=0))
            return tuple(result)

        sums = lax.fori_loop(0, count, weigh, tuple(jnp.zeros((8, 256), F32) for _ in range(4)))
        for h in range(4):
            share = 1.0 / jnp.sum(sums[h], axis=0, keepdims=True)
            for half in range(2):
                part_share = share[:, half * 128 : half * 128 + 128]
                start = h * 256 + half * 128
                grad = side[qx * 2 + half, 384 + h * 96 : 480 + h * 96, :]
                DO[0:96, start : start + 128] = (grad.astype(F32) * part_share).astype(BF16)
                d = side[qx * 2 + half, 768:784, :].astype(F32)
                d = -(d[h : h + 1] + d[4 + h : 5 + h] + d[8 + h : 9 + h]) * part_share
                high, middle, low = split3(d)
                DO[96:128, start : start + 128] = jnp.where(
                    row_id == 0, high, jnp.where(row_id == 1, middle, jnp.where(row_id == 2, low, 0.0))
                ).astype(BF16)
        DQ[...] = jnp.zeros((96, 1024), F32)

        def gradient(kb, _):
            pieces = []
            for h in range(4):
                lanes = slice(h * 256, h * 256 + 256)
                dp = jnp.dot(Vn[kb], DO[:, lanes], preferred_element_type=F32)
                pieces.append((Pm[kb, :, lanes].astype(F32) * dp).astype(BF16))
            ds = jnp.concatenate(pieces, axis=1)
            dVa[kb] += lax.dot_general(DO[0:96, :], Pm[kb], NT, preferred_element_type=F32)
            dKa[kb] += lax.dot_general(QT[0:96, :], ds, NT, preferred_element_type=F32)
            DQ[...] += jnp.dot(KT[kb], ds, preferred_element_type=F32)
            return 0

        lax.fori_loop(0, count, gradient, 0)
        for h in range(4):
            for half in range(2):
                start = h * 256 + half * 128
                dq_src[qx * 2 + half, h * 96 : h * 96 + 96, :] = (
                    DQ[:, start : start + 128] * SCALE
                ).astype(BF16)
        return 0

    lax.fori_loop(0, 4, query_block, 0)
    for half in range(2):
        lanes = slice(half * 128, half * 128 + 128)

        def finish(i, _):
            b = i // 4
            px = i % 4
            part[b, half, px, 0:96, :] = (dKa[px * 4 + b, :, lanes] * LN2).astype(BF16)
            part[b, half, px, 96:192, :] = dVa[px * 4 + b, :, lanes].astype(BF16)
            return 0

        lax.fori_loop(0, 16, finish, 0)

    moved = []
    for p in peers:
        copy = remote(dq_src.at[p], dq_out.at[mine], s_dq.at[p], r_dq.at[mine], at(p // 2, z, p % 2))
        copy.start()
        moved.append(copy)
    order = (3, 0, 2, 1)
    swaps = {}
    for b in order:
        swaps[b] = remote(part.at[b, 1 - c], core_in.at[b], s_pc.at[b], r_pc.at[b], at(x, z, 1 - c))
        swaps[b].start()
    dq_out[mine] = dq_src[mine]
    for b in order:
        swaps[b].wait()

        def add(i, _):
            part[b, c, i] = (part[b, c, i].astype(F32) + core_in[b, i].astype(F32)).astype(BF16)
            return 0

        lax.fori_loop(0, 4, add, 0)

    def pass_right(t):
        return remote(total_r.at[t], total_r.at[t], s_tr.at[t], r_tr.at[t], at(x, z + 1, c))

    def pass_left(t):
        return remote(total_l.at[t], total_l.at[t], s_tl.at[t], r_tl.at[t], at(x, z - 1, c))

    def hop(total, t, first, descriptor):
        @pl.when(first)
        def _():
            total[t] = part[t, c]

        @pl.when(jnp.logical_not(first))
        def _():
            descriptor(t).wait_recv()

            def add(i, _):
                total[t, i] = (total[t, i].astype(F32) + part[t, c, i].astype(F32)).astype(BF16)
                return 0

            lax.fori_loop(0, 4, add, 0)

        descriptor(t).start()

    for right, left in ((3, 0), (2, 1), (1, 2)):
        @pl.when(z < right)
        def _():
            hop(total_r, right, z == 0, pass_right)

        @pl.when(z > left)
        def _():
            hop(total_l, left, z == 3, pass_left)

    def gather(i, _):
        final[i] = part[z, c, i].astype(F32)
        return 0

    lax.fori_loop(0, 4, gather, 0)

    @pl.when(z > 0)
    def _():
        pass_right(z).wait_recv()

        def add(i, _):
            final[i] += total_r[z, i].astype(F32)
            return 0

        lax.fori_loop(0, 4, add, 0)

    @pl.when(z < 3)
    def _():
        pass_left(z).wait_recv()

        def add(i, _):
            final[i] += total_l[z, i].astype(F32)
            return 0

        lax.fori_loop(0, 4, add, 0)

    def settle(i, _):
        core_in[0, i] = final[i].astype(BF16)
        return 0

    lax.fori_loop(0, 4, settle, 0)
    sent = []
    for j in range(1, 4):
        px = lax.rem(x + j, 4)
        copy = remote(core_in.at[0, px], dkv_out.at[x], s_f.at[j], r_f.at[x], at(px, z, c))
        copy.start()
        sent.append(copy)
    dkv_out[x] = core_in[0, x]
    for t in range(4):
        @pl.when(z < t)
        def _():
            pass_right(t).wait_send()

        @pl.when(z > t)
        def _():
            pass_left(t).wait_send()

    for p, copy in zip(peers, moved):
        remote(dq_src.at[p], dq_out.at[p], s_dq.at[p], r_dq.at[p], at(p // 2, z, p % 2)).wait_recv()
        copy.wait_send()
    for j, copy in zip(range(1, 4), sent):
        px = lax.rem(x + j, 4)
        remote(core_in.at[0, px], dkv_out.at[px], s_f.at[j], r_f.at[px], at(px, z, c)).wait_recv()
        copy.wait_send()


def finish_kernel(group_ref, dq_ref, dkv_ref, q_ref, k_ref, v_ref, qt, kt, vt, slot_ref, count_ref):
    find_slots(group_ref, slot_ref, count_ref)

    def one_head(h, _):
        slot = slot_ref[h]
        place = pl.multiple_of((slot % 4) * WIDTH, 32)
        qt[pl.ds(pl.multiple_of(h * WIDTH, 32), WIDTH), :] = dq_ref[slot // 4, pl.ds(place, WIDTH), :]
        return 0

    lax.fori_loop(0, HEADS, one_head, 0)
    for g in range(GROUPS):
        kt[g * WIDTH : (g + 1) * WIDTH, :] = dkv_ref[g, 0:96, :]
        vt[g * WIDTH : (g + 1) * WIDTH, :] = dkv_ref[g, 96:192, :]

    def flip(j, _):
        lanes = pl.ds(pl.multiple_of(j * 128, 128), 128)
        q_ref[:, lanes] = qt[lanes, :].T
        return 0

    lax.fori_loop(0, 24, flip, 0)
    for j in range(3):
        lanes = slice(j * 128, j * 128 + 128)
        k_ref[:, lanes] = kt[lanes, :].T
        v_ref[:, lanes] = vt[lanes, :].T


def per_device(queries, key_states, value_states, outputs, out_grad, window_start, head_group):
    in_vmem = pl.BlockSpec(memory_space=VM)
    in_smem = pl.BlockSpec(memory_space=pltpu.SMEM)
    shape = jax.ShapeDtypeStruct
    me = lax.axis_index("seq")
    position = (window_start[0] + me * 128 + jnp.arange(128, dtype=jnp.int32)).astype(F32)
    half = ROT_DIM // 2
    frequency = 10000.0 ** (-2.0 * jnp.arange(half, dtype=F32) / ROT_DIM)
    angles = position[None, :] * frequency[:, None]
    cosine, sine = jnp.cos(angles), jnp.sin(angles)
    turn = jnp.stack([jnp.concatenate([cosine, cosine], 0), jnp.concatenate([-sine, sine], 0)])
    smem = pltpu.SMEM
    side, kv = pl.pallas_call(
        prep_kernel,
        out_shape=(shape((8, SIDE_ROWS, 128), BF16), shape((4, 192, 128), BF16)),
        in_specs=[in_smem] + [in_vmem] * 6,
        out_specs=(in_vmem, in_vmem),
        scratch_shapes=[VM((3072, 128), BF16)] * 3 + [VM((384, 128), BF16)] * 2
        + [VM((32, 128), F32), smem((32,), jnp.int32), smem((4,), jnp.int32)],
        compiler_params=pltpu.CompilerParams(vmem_limit_bytes=24 << 20),
    )(head_group, queries, key_states, value_states, outputs, out_grad, turn)
    dma = pltpu.SemaphoreType.DMA
    dq, dkv = pl.pallas_call(
        main_kernel,
        out_shape=(shape((8, 384, 128), BF16), shape((4, 192, 128), BF16)),
        in_specs=[in_vmem] * 2,
        out_specs=(in_vmem, in_vmem),
        scratch_shapes=[
            VM((8, SIDE_ROWS, 128), BF16), VM((4, 2, 4, 192, 128), BF16),
            VM((16, 256, 1024), F32), VM((16, 256, 1024), BF16),
            VM((128, 1024), BF16), VM((128, 1024), BF16),
            VM((16, 256, 128), BF16), VM((16, 256, 128), BF16), VM((16, 96, 256), BF16),
            VM((16, 96, 256), F32), VM((16, 96, 256), F32), VM((96, 1024), F32),
            VM((8, 384, 128), BF16), VM((4, 2, 4, 192, 128), BF16), VM((4, 4, 192, 128), BF16),
            VM((4, 4, 192, 128), BF16), VM((4, 4, 192, 128), BF16), VM((4, 192, 128), F32),
        ] + [dma((8,))] * 2 + [dma((4,))] * 8 + [dma((8,))] * 2 + [dma((4,))] * 8,
        compiler_params=pltpu.CompilerParams(
            collective_id=0, has_side_effects=True, vmem_limit_bytes=60 << 20
        ),
    )(side, kv)
    return pl.pallas_call(
        finish_kernel,
        out_shape=(shape((128, 3072), BF16), shape((128, 384), BF16), shape((128, 384), BF16)),
        in_specs=[in_smem, in_vmem, in_vmem],
        out_specs=(in_vmem, in_vmem, in_vmem),
        scratch_shapes=[VM((3072, 128), BF16)] + [VM((384, 128), BF16)] * 2
        + [smem((32,), jnp.int32), smem((4,), jnp.int32)],
        compiler_params=pltpu.CompilerParams(vmem_limit_bytes=24 << 20),
    )(head_group, dq, dkv)


def solution(mesh):
    rows = P(("dp", "seq"), None)
    return jax.shard_map(
        per_device,
        mesh=mesh,
        in_specs=(rows, rows, rows, rows, rows, P("dp"), P()),
        out_specs=(rows, rows, rows),
        check_vma=False,
    )
```

time: 362 us -> 124 us (0.34)
  waiting for transfers between devices: 181 us -> 0 us
  Pallas kernels: 0 us -> 110 us
  matrix products: 81.7 us -> 0 us
  starting transfers between devices: 32.7 us -> 0 us
  local copies, waits for them, and re-layouts: 29.9 us -> 9.74 us
  other arithmetic: 17.9 us -> 0.15 us
  between operations: 15.6 us -> 1.37 us
    all_to_all x6 -> x0, waiting for transfers between devices: 129 us -> none  [the longest x1 24.2 us: per_device(): lax.all_to_all(out_grad, 'seq', split_axis=1, concat_axis=0, tiled=True)]
    pallas_call x0 -> x3, Pallas kernels: none -> 110 us  [the longest x1 103 us: per_device(): pl.pallas_call(main_kernel, out_shape=(shape((8, 384, 128), BF16), shape(...]
    dot_general x62 -> x0, matrix products: 81.7 us -> none  [the longest x10 30.1 us: gradient(): lax.dot_general(weights_half, grad_rows, contract_first, preferred_elemen...]
    all_gather x2 -> x0, waiting for transfers between devices: 51.9 us -> none  [the longest x1 51.9 us: per_device(): lax.all_gather(value_states, 'seq', axis=0, tiled=True)]
    all_to_all x6 -> x0, starting transfers between devices: 32.6 us -> none  [the longest x1 10.2 us: per_device(): lax.all_to_all(query_rot, 'seq', split_axis=1, concat_axis=0, tiled=True)]
    dynamic_slice x11 -> x0, local copies, waits for them, and re-layouts: 11.7 us -> none  [the longest x4 4.25 us: outer(): grad_rows = lax.dynamic_slice_in_dim(grad_head, query_start, block_size, 0)]
    reduce_sum x11 -> x0, other arithmetic: 11.1 us -> none  [the longest x10 10.3 us: statistic(): jnp.sum(jnp.exp(scores - new_max[:, None]), axis=1)]
    all_to_all x3 -> x0, other arithmetic: 4.52 us -> none  [the longest x1 2.46 us: per_device(): lax.all_to_all(query_half, 'seq', split_axis=0, concat_axis=1, tiled=True)]
  transfers between devices with their start and end apart: 8 -> 0, of which waited for: 7 -> 0; matrix products, arithmetic and copies ran while one was open for 5% -> 0% of each run, Pallas kernels for 0% -> 0%
where the time goes in v1:
time: 124 us; the launch traced here: 121 us
  Pallas kernels  110 us (89%)
  local copies, waits for them, and re-layouts  9.74 us (8%)
  between operations  1.37 us (1%)
    pallas_call x1, Pallas kernels, per_device(): pl.pallas_call(main_kernel, out_shape=(shape((8, 384, 128), BF16), shape(...  103 us
    unnamed x22, local copies, waits for them, and re-layouts  9.74 us
    pallas_call x1, Pallas kernels, per_device(): pl.pallas_call(prep_kernel, out_shape=(shape((8, SIDE_ROWS, 128), BF16),...  3.81 us
    pallas_call x1, Pallas kernels, per_device(): pl.pallas_call(finish_kernel, out_shape=(shape((128, 3072), BF16), shape(...  3.8 us

profile of v1, /device:TPU:1, one launch (start us, length us, event | category | flops | bytes accessed | tf_op | source)
XLA Modules:
  0.0 121.5 jit_solution(6287816127638489935)
XLA Ops:
  1.3 0.1 multiply_cosine_fusion
  1.5 0.0 copy-start.2
  1.5 1.1 copy-done.2
  2.6 0.0 copy-start.3
  2.6 1.1 copy-done.3
  3.7 0.0 copy-start.4
  3.7 1.1 copy-done.4
  4.9 0.0 copy-start.7
  4.9 0.9 copy-done.7
  5.8 0.0 copy-start.8
  5.8 0.9 copy-done.8
  6.7 0.0 copy-start.9
  6.7 0.7 copy-done.9
  7.3 0.0 copy-start.10
  7.3 3.8 %shard_map.94 = (bf16[8,784,128]{2,1,0:T(8,128)(2,1)S(1)}, bf16[4,192,128]{2,1,0:T(8,128)(2,1)S(1)}) custom-call(s32[32]{0:T(128)S(1)} %copy-done.9, bf16[128,3072]{1,0:T(8,128)(2,1)S(1)} %copy-done.2, bf16[128,384]{1,0:T(8,128)(2,1)S(1)} %copy-done.7, bf16[128,384]{1,0:T(8,128)(2,1)S(1)} %copy-done.8, bf16[128,3072]{1,0:T(8,128)(2,1)S(1)} %copy-done.3, ...), custom_call_target="tpu_custom_call" | custom-call | tf_op jit(solution)/shard_map/pallas_call | solution.py:469
  11.1 0.0 copy-start
  11.1 1.2 copy-done
  12.3 0.7 copy-done.6
  13.0 102.6 %shard_map.95 = (bf16[8,384,128]{2,1,0:T(8,128)(2,1)}, bf16[4,192,128]{2,1,0:T(8,128)(2,1)}) custom-call(bf16[8,784,128]{2,1,0:T(8,128)(2,1)} %copy-done, bf16[4,192,128]{2,1,0:T(8,128)(2,1)} %copy-done.6), custom_call_target="tpu_custom_call" | custom-call | tf_op jit(solution)/shard_map/pallas_call | solution.py:479
  115.6 0.0 copy-done.10
  115.6 0.0 copy-start.1
  115.6 1.1 copy-done.1
  116.8 0.9 copy-done.5
  117.7 3.8 %shard_map.96 = (bf16[128,3072]{1,0:T(8,128)(2,1)}, bf16[128,384]{1,0:T(8,128)(2,1)}, bf16[128,384]{1,0:T(8,128)(2,1)}) custom-call(s32[32]{0:T(128)S(1)} %copy-done.10, bf16[8,384,128]{2,1,0:T(8,128)(2,1)S(1)} %copy-done.1, bf16[4,192,128]{2,1,0:T(8,128)(2,1)S(1)} %copy-done.5), custom_call_target="tpu_custom_call" | custom-call | tf_op jit(solution)/shard_map/pallas_call | solution.py:497
  (6 shorter events, 0.0 us)
Async XLA Ops:
  1.5 1.1 copy-start.2
  2.6 1.1 copy-start.3
  3.7 1.1 copy-start.4
  4.9 0.9 copy-start.7
  5.8 0.9 copy-start.8
  6.7 0.7 copy-start.9
  7.3 108.3 %copy-start.10 = (s32[32]{0:T(128)S(1)}, s32[32]{0:T(128)}, u32[]{:S(2)}) copy-start(s32[32]{0:T(128)} %group_ref.3) | copy-start | bytes 388
  11.1 1.2 copy-start
  12.3 0.7 copy-start.6
  115.6 1.1 copy-start.1
  116.8 0.9 copy-start.5

commit v2 on v0

v2 whole, which is shorter than its diff:
```python
import math

import jax
import jax.numpy as jnp
from jax import lax
from jax.experimental import pallas as pl
from jax.experimental.pallas import tpu as pltpu
from jax.sharding import PartitionSpec as P

HEADS = 32
GROUPS = 4
WIDTH = 96
ROT_DIM = 24
F32 = jnp.float32
BF16 = jnp.bfloat16
LN2 = math.log(2.0)
SCALE = WIDTH**-0.5
NT = (((1,), (1,)), ((), ()))
VM = pltpu.VMEM
GRAD_ROWS = 400


def split3(value):
    high = value.astype(BF16)
    rest = value - high.astype(F32)
    middle = rest.astype(BF16)
    low = (rest - middle.astype(F32)).astype(BF16)
    return high.astype(F32), middle.astype(F32), low.astype(F32)


def kernel(perm, slot_of, turn, q_hbm, k_hbm, v_hbm, o_hbm, g_hbm, dq_hbm, dk_hbm, dv_hbm,
           q_in, g_in, o_in, k_in, v_in, qt, gt, ot, kt, vt, dq_buf, dk_buf, dv_buf,
           ksrc, vsrc, kin, vin, qsrc, gsrc, qin, gin,
           S, bias, Pm, D, QT, DO, Kn, Vn, KT, dKa, dVa, DQ, mrun, mfin, share,
           dq_src, dq_in, part, cin, zin, tot, fin,
           s_in, s_out, s_q, r_q, s_g, r_g, s_kx, r_kx, s_vx, r_vx, s_kz, r_kz, s_kc, r_kc,
           s_vz, r_vz, s_vc, r_vc, s_d, r_d, s_p, r_p, s_z, r_z, s_f, r_f):
    me = lax.axis_index("seq")
    x = me // 8
    z = (me // 2) % 4
    c = me % 2
    mine = x * 2 + c
    mesh_id = pl.DeviceIdType.MESH
    mult = pl.multiple_of

    def at(px, pz, pc):
        return {"seq": px * 8 + pz * 2 + pc}

    def owner_at(p):
        return at(p // 2, z, p % 2)

    def remote(src, dst, send, recv, where):
        return pltpu.make_async_remote_copy(
            src_ref=src, dst_ref=dst, send_sem=send, recv_sem=recv,
            device_id=where, device_id_type=mesh_id,
        )

    def loads():
        pairs = ((k_hbm, k_in), (v_hbm, v_in), (q_hbm, q_in), (g_hbm, g_in), (o_hbm, o_in))
        return [pltpu.make_async_copy(a, b, s_in.at[i]) for i, (a, b) in enumerate(pairs)]

    incoming = loads()
    for copy in incoming:
        copy.start()
    barrier = pltpu.get_barrier_semaphore()
    for j in range(1, 8):
        pl.semaphore_signal(barrier, inc=1, device_id=owner_at(lax.rem(mine + j, 8)), device_id_type=mesh_id)
    for j in range(1, 4):
        pl.semaphore_signal(barrier, inc=1, device_id=at(x, lax.rem(z + j, 4), c), device_id_type=mesh_id)

    cosine = turn[0]
    sine = turn[1]

    def turned(rows):
        first = rows[0:ROT_DIM]
        swapped = jnp.concatenate([first[12:24], first[0:12]], axis=0)
        return jnp.concatenate([first * cosine + swapped * sine, rows[ROT_DIM:]], axis=0)

    def k_along_x(px, land):
        return remote(ksrc.at[px], kin.at[z, c, land], s_kx.at[px], r_kx.at[land], at(px, z, c))

    def v_along_x(px, land):
        return remote(vsrc.at[px], vin.at[z, c, land], s_vx.at[px], r_vx.at[land], at(px, z, c))

    def k_along_z(px, pz, land):
        return remote(kin.at[land, c, px], kin.at[land, c, px], s_kz.at[px * 4 + pz],
                      r_kz.at[px * 4 + land], at(x, pz, c))

    def k_to_core(px, land):
        return remote(kin.at[:, land, px], kin.at[:, land, px], s_kc.at[px], r_kc.at[px], at(x, z, 1 - c))

    def v_along_z(pz, land):
        return remote(vin.at[land, c], vin.at[land, c], s_vz.at[pz], r_vz.at[land], at(x, pz, c))

    def v_to_core(land):
        return remote(vin.at[:, land], vin.at[:, land], s_vc.at[0], r_vc.at[0], at(x, z, 1 - c))

    def q_move(p, land):
        return remote(qsrc.at[p], qin.at[land], s_q.at[p], r_q.at[land], owner_at(p))

    def g_move(p, land):
        return remote(gsrc.at[p], gin.at[land], s_g.at[p], r_g.at[land], owner_at(p))

    def dq_move(p, land):
        return remote(dq_src.at[p], dq_in.at[pl.ds(land * 4, 4)], s_d.at[p], r_d.at[land], owner_at(p))

    def part_move(px):
        return remote(part.at[px, 1 - c], cin.at[px], s_p.at[px], r_p.at[px], at(x, z, 1 - c))

    def sum_along_z(px, pz, land):
        return remote(part.at[px, c, pz], zin.at[px, land], s_z.at[px * 4 + pz], r_z.at[px * 4 + land], at(x, pz, c))

    def total_move(px, land):
        return remote(tot.at[px], fin.at[land], s_f.at[px], r_f.at[land], at(px, z, c))

    def over_x(action):
        for j in range(1, 4):
            action(lax.rem(x + j, 4))

    def over_z(action):
        for j in range(1, 4):
            action(lax.rem(z + j, 4))

    incoming[0].wait()
    for j in range(3):
        lanes = slice(j * 128, j * 128 + 128)
        kt[lanes, :] = k_in[:, lanes].T
    for g in range(GROUPS):
        ksrc[g] = turned(kt[g * WIDTH : (g + 1) * WIDTH, :].astype(F32)).astype(BF16)
    pl.semaphore_wait(barrier, 10)
    over_x(lambda px: k_along_x(px, x).start())
    kin[z, c, x] = ksrc[x]
    incoming[1].wait()
    for j in range(3):
        lanes = slice(j * 128, j * 128 + 128)
        vt[lanes, :] = v_in[:, lanes].T
    for g in range(GROUPS):
        vsrc[g] = vt[g * WIDTH : (g + 1) * WIDTH, :]

    incoming[2].wait()

    def flip_q(j, _):
        rows = q_in[:, pl.ds(mult(j * 384, 128), 384)].T
        for i in range(4):
            qt[j * 4 + i] = rows[i * WIDTH : (i + 1) * WIDTH]
        return 0

    lax.fori_loop(0, 8, flip_q, 0)

    def send_q(j, _):
        p = lax.rem(mine + j, 8)
        for i in range(4):
            rows = qt[perm[p * 4 + i]]
            qsrc[p, i * WIDTH : (i + 1) * WIDTH, :] = (turned(rows.astype(F32)) * (SCALE / LN2)).astype(BF16)

        @pl.when(j < 8)
        def _():
            q_move(p, mine).start()

        return 0

    lax.fori_loop(1, 9, send_q, 0)
    qin[mine] = qsrc[mine]

    over_x(lambda px: k_along_x(px, px).wait_recv())

    def spread_k(px, _):
        over_z(lambda pz: k_along_z(px, pz, z).start())
        return 0

    lax.fori_loop(0, 4, spread_k, 0)
    over_x(lambda px: v_along_x(px, x).start())
    vin[z, c, x] = vsrc[x]

    incoming[3].wait()
    incoming[4].wait()

    def flip_g(j, _):
        lanes = pl.ds(mult(j * 384, 128), 384)
        grads = g_in[:, lanes].T
        outs = o_in[:, lanes].T
        for i in range(4):
            gt[j * 4 + i] = grads[i * WIDTH : (i + 1) * WIDTH]
            ot[j * 4 + i] = outs[i * WIDTH : (i + 1) * WIDTH]
        return 0

    lax.fori_loop(0, 8, flip_g, 0)

    def send_g(j, _):
        p = lax.rem(mine + j, 8)
        deltas = []
        for i in range(4):
            head = perm[p * 4 + i]
            grad = gt[head]
            gsrc[p, i * WIDTH : (i + 1) * WIDTH, :] = grad
            deltas.append(jnp.sum(grad.astype(F32) * ot[head].astype(F32), axis=0, keepdims=True))
        high, middle, low = split3(jnp.concatenate(deltas, axis=0))
        gsrc[p, 384:400, :] = jnp.concatenate(
            [high, middle, low, jnp.zeros((4, 128), F32)], axis=0
        ).astype(BF16)

        @pl.when(j < 8)
        def _():
            g_move(p, mine).start()

        return 0

    lax.fori_loop(1, 9, send_g, 0)
    gin[mine] = gsrc[mine]

    def make_bias(i, _):
        rows = pl.ds(mult(i * 256, 256), 256)
        key_id = lax.broadcasted_iota(jnp.int32, (256, 256), 0) + (i - z) * 256
        bias[rows, :] = jnp.where(key_id <= lax.broadcasted_iota(jnp.int32, (256, 256), 1), 0.0, -1e30)
        return 0

    lax.fori_loop(0, 4, make_bias, 0)

    def clear(i, _):
        dKa[i] = jnp.zeros((96, 1024), F32)
        dVa[i] = jnp.zeros((96, 1024), F32)
        return 0

    lax.fori_loop(0, 4, clear, 0)
    QT[96:128, :] = jnp.zeros((32, 1024), BF16)

    def share_k(px, _):
        over_z(lambda pz: k_along_z(px, pz, pz).wait_recv())
        k_to_core(px, c).start()
        return 0

    lax.fori_loop(0, 4, share_k, 0)
    over_x(lambda px: v_along_x(px, px).wait_recv())
    over_z(lambda pz: v_along_z(pz, z).start())

    heads = [slice(h * 256, h * 256 + 256) for h in range(4)]
    one_rows = (lax.broadcasted_iota(jnp.int32, (32, 128), 0) < 3).astype(BF16)
    zero_rows = jnp.zeros((32, 128), BF16)

    def load_queries(qx):
        for h in range(4):
            for half in range(2):
                start = h * 256 + half * 128
                QT[0:96, start : start + 128] = qin[qx * 2 + half, h * 96 : h * 96 + 96, :]

    def weights_of(qx, _):
        k_to_core(qx, 1 - c).wait_recv()
        for half in range(2):
            p = qx * 2 + half

            @pl.when(p != mine)
            def _():
                q_move(p, p).wait_recv()

        for b in range(8):
            lanes = slice(b * 128, b * 128 + 128)
            keys = kin[b // 2, b % 2, qx]
            KT[qx, :, lanes] = keys
            Kn[qx, lanes, :] = jnp.concatenate([keys, zero_rows], 0).T
        load_queries(qx)
        first = qx * (qx + 1) // 2

        def block(px, state, diagonal):
            top, total = state[:4], state[4:]
            new_top, new_total = [], []
            for h in range(4):
                s = jnp.dot(Kn[px], QT[:, heads[h]], preferred_element_type=F32)
                if diagonal:
                    s = s + bias[...]
                S[:, heads[h]] = s
                high = jnp.max(jnp.max(s.reshape(128, 8, 256), axis=0), axis=0, keepdims=True)
                new_top.append(jnp.maximum(top[h], high))
            for h in range(4):
                p = jnp.exp2(S[:, heads[h]] - new_top[h])
                Pm[first + px, :, heads[h]] = p.astype(BF16)
                new_total.append(
                    total[h] * jnp.exp2(top[h] - new_top[h]) + jnp.sum(p.reshape(128, 8, 256), axis=0)
                )
                mrun[first + px, :, heads[h]] = new_top[h]
            return tuple(new_top) + tuple(new_total)

        state = tuple(jnp.full((1, 256), -1e30, F32) for _ in range(4)) + tuple(
            jnp.zeros((8, 256), F32) for _ in range(4)
        )
        state = lax.fori_loop(0, qx, lambda px, st: block(px, st, False), state)
        state = block(qx, state, True)
        for h in range(4):
            mfin[qx, :, heads[h]] = state[h]
            share[qx, :, heads[h]] = 1.0 / jnp.sum(state[4 + h], axis=0, keepdims=True)

        @pl.when(qx == 2)
        def _():
            over_z(lambda pz: v_along_z(pz, pz).wait_recv())
            v_to_core(c).start()

        return 0

    lax.fori_loop(0, 4, weights_of, 0)
    v_to_core(1 - c).wait_recv()

    def stage_v(px, _):
        for b in range(8):
            lanes = slice(b * 128, b * 128 + 128)
            Vn[px, lanes, :] = jnp.concatenate([vin[b // 2, b % 2, px], one_rows], 0).T
        return 0

    lax.fori_loop(0, 4, stage_v, 0)
    row_id = lax.broadcasted_iota(jnp.int32, (32, 128), 0)

    def reduce_cores(px):
        part_move(px).wait()

        def add(b, _):
            part[px, c, b] = (part[px, c, b].astype(F32) + cin[px, b].astype(F32)).astype(BF16)
            return 0

        lax.fori_loop(0, 4, add, 0)
        over_z(lambda pz: sum_along_z(px, pz, z).start())

    def reduce_z(px):
        over_z(lambda pz: sum_along_z(px, pz, pz).wait_recv())
        value = part[px, c, z].astype(F32)
        for j in range(1, 4):
            value = value + zin[px, lax.rem(z + j, 4)].astype(F32)
        tot[px] = value.astype(BF16)

        @pl.when(px != x)
        def _():
            total_move(px, x).start()

        @pl.when(px == x)
        def _():
            fin[x] = tot[px]

    def gradients_of(i, _):
        qx = 3 - i
        for half in range(2):
            p = qx * 2 + half

            @pl.when(p != mine)
            def _():
                g_move(p, p).wait_recv()

        load_queries(qx)
        DQ[...] = jnp.zeros((96, 1024), F32)
        first = qx * (qx + 1) // 2

        def block(px, _):
            factor = jnp.exp2(mrun[first + px] - mfin[qx]) * share[qx]
            for h in range(4):
                for half in range(2):
                    start = h * 256 + half * 128
                    scale = factor[:, start : start + 128]
                    grad = gin[qx * 2 + half, h * 96 : h * 96 + 96, :]
                    DO[0:96, start : start + 128] = (grad.astype(F32) * scale).astype(BF16)
                    d = gin[qx * 2 + half, 384:400, :].astype(F32)
                    d = -(d[h : h + 1] + d[4 + h : 5 + h] + d[8 + h : 9 + h]) * scale
                    high, middle, low = split3(d)
                    DO[96:128, start : start + 128] = jnp.where(
                        row_id == 0, high, jnp.where(row_id == 1, middle, jnp.where(row_id == 2, low, 0.0))
                    ).astype(BF16)
            for h in range(4):
                for r in range(4):
                    rows = slice(r * 256, r * 256 + 256)
                    dp = jnp.dot(Vn[px, rows, :], DO[:, heads[h]], preferred_element_type=F32)
                    D[rows, heads[h]] = (Pm[first + px, rows, heads[h]].astype(F32) * dp).astype(BF16)
                dVa[px] += lax.dot_general(DO[0:96, heads[h]], Pm[first + px, :, heads[h]], NT,
                                           preferred_element_type=F32)
                dKa[px] += lax.dot_general(QT[0:96, heads[h]], D[:, heads[h]], NT, preferred_element_type=F32)
                DQ[:, heads[h]] += jnp.dot(KT[px], D[:, heads[h]], preferred_element_type=F32)
            return 0

        lax.fori_loop(0, qx + 1, block, 0)
        for half in range(2):
            p = qx * 2 + half
            for h in range(4):
                start = h * 256 + half * 128
                dq_src[p, h] = (DQ[:, start : start + 128] * SCALE).astype(BF16)

            @pl.when(p != mine)
            def _():
                dq_move(p, mine).start()

        for b in range(8):
            lanes = slice(b * 128, b * 128 + 128)
            part[qx, b % 2, b // 2, 0:96, :] = (dKa[qx, :, lanes] * LN2).astype(BF16)
            part[qx, b % 2, b // 2, 96:192, :] = dVa[qx, :, lanes].astype(BF16)
        part_move(qx).start()

        @pl.when(i >= 1)
        def _():
            reduce_cores(qx + 1)

        @pl.when(i >= 2)
        def _():
            reduce_z(qx + 2)

        return 0

    lax.fori_loop(0, 4, gradients_of, 0)
    reduce_cores(0)

    dq_in[pl.ds(mine * 4, 4)] = dq_src[mine]

    def arrive_dq(j, _):
        p = lax.rem(mine + j, 8)
        dq_move(p, p).wait_recv()
        return 0

    lax.fori_loop(1, 8, arrive_dq, 0)
    reduce_z(1)

    def flip_back(j, _):
        rows = jnp.concatenate([dq_in[slot_of[j * 4 + i]] for i in range(4)], axis=0)
        dq_buf[:, pl.ds(mult(j * 384, 128), 384)] = rows.T
        return 0

    lax.fori_loop(0, 8, flip_back, 0)
    outgoing = [pltpu.make_async_copy(dq_buf, dq_hbm, s_out.at[0])]
    outgoing[0].start()
    reduce_z(0)
    over_x(lambda px: total_move(px, px).wait_recv())
    for g in range(GROUPS):
        kt[g * WIDTH : (g + 1) * WIDTH, :] = fin[g, 0:96, :]
        vt[g * WIDTH : (g + 1) * WIDTH, :] = fin[g, 96:192, :]
    for j in range(3):
        lanes = slice(j * 128, j * 128 + 128)
        dk_buf[:, lanes] = kt[lanes, :].T
        dv_buf[:, lanes] = vt[lanes, :].T
    outgoing.append(pltpu.make_async_copy(dk_buf, dk_hbm, s_out.at[1]))
    outgoing.append(pltpu.make_async_copy(dv_buf, dv_hbm, s_out.at[2]))
    outgoing[1].start()
    outgoing[2].start()

    def sent(p):
        q_move(p, mine).wait_send()
        g_move(p, mine).wait_send()
        dq_move(p, mine).wait_send()

    def sent_all(j, _):
        sent(lax.rem(mine + j, 8))
        return 0

    lax.fori_loop(1, 8, sent_all, 0)

    def sent_x(px):
        k_along_x(px, x).wait_send()
        v_along_x(px, x).wait_send()
        total_move(px, x).wait_send()

    over_x(sent_x)
    over_z(lambda pz: v_along_z(pz, z).wait_send())
    v_to_core(c).wait_send()

    def sent_z(px, _):
        over_z(lambda pz: k_along_z(px, pz, z).wait_send())
        over_z(lambda pz: sum_along_z(px, pz, z).wait_send())
        k_to_core(px, c).wait_send()
        return 0

    lax.fori_loop(0, 4, sent_z, 0)
    for copy in outgoing:
        copy.wait()


def per_device(queries, key_states, value_states, outputs, out_grad, window_start, head_group):
    in_vmem = pl.BlockSpec(memory_space=VM)
    in_smem = pl.BlockSpec(memory_space=pltpu.SMEM)
    anywhere = pl.BlockSpec(memory_space=pl.ANY)
    shape = jax.ShapeDtypeStruct
    me = lax.axis_index("seq")
    position = (window_start[0] + me * 128 + jnp.arange(128, dtype=jnp.int32)).astype(F32)
    half = ROT_DIM // 2
    frequency = 10000.0 ** (-2.0 * jnp.arange(half, dtype=F32) / ROT_DIM)
    angles = position[None, :] * frequency[:, None]
    cosine, sine = jnp.cos(angles), jnp.sin(angles)
    turn = jnp.stack([jnp.concatenate([cosine, cosine], 0), jnp.concatenate([-sine, sine], 0)])
    ids = jnp.arange(HEADS, dtype=jnp.int32)
    same = (head_group[:, None] == head_group[None, :]) & (ids[None, :] < ids[:, None])
    slot_of = head_group * 8 + jnp.sum(same.astype(jnp.int32), axis=1)
    perm = jnp.sum(jnp.where(slot_of[:, None] == ids[None, :], ids[:, None], 0), axis=0)
    dma = pltpu.SemaphoreType.DMA
    wide = VM((128, 3072), BF16)
    tall = VM((HEADS, WIDTH, 128), BF16)
    small = VM((128, 384), BF16)
    small_t = VM((384, 128), BF16)
    return pl.pallas_call(
        kernel,
        out_shape=(shape((128, 3072), BF16), shape((128, 384), BF16), shape((128, 384), BF16)),
        in_specs=[in_smem, in_smem, in_vmem] + [anywhere] * 5,
        out_specs=(anywhere, anywhere, anywhere),
        scratch_shapes=[
            wide, wide, wide, small, small, tall, tall, tall, small_t, small_t, wide, small, small,
            VM((4, 96, 128), BF16), VM((4, 96, 128), BF16),
            VM((4, 2, 4, 96, 128), BF16), VM((4, 2, 4, 96, 128), BF16),
            VM((8, 384, 128), BF16), VM((8, GRAD_ROWS, 128), BF16),
            VM((8, 384, 128), BF16), VM((8, GRAD_ROWS, 128), BF16),
            VM((1024, 1024), F32), VM((1024, 256), F32), VM((10, 1024, 1024), BF16), VM((1024, 1024), BF16),
            VM((128, 1024), BF16), VM((128, 1024), BF16),
            VM((4, 1024, 128), BF16), VM((4, 1024, 128), BF16), VM((4, 96, 1024), BF16),
            VM((4, 96, 1024), F32), VM((4, 96, 1024), F32), VM((96, 1024), F32),
            VM((10, 1, 1024), F32), VM((4, 1, 1024), F32), VM((4, 1, 1024), F32),
            VM((8, 4, 96, 128), BF16), VM((32, 96, 128), BF16),
            VM((4, 2, 4, 192, 128), BF16), VM((4, 4, 192, 128), BF16), VM((4, 4, 192, 128), BF16),
            VM((4, 192, 128), BF16), VM((4, 192, 128), BF16),
        ]
        + [dma((n,)) for n in (5, 3, 8, 8, 8, 8, 4, 4, 4, 4, 16, 16, 4, 4, 4, 4, 1, 1, 8, 8, 4, 4, 16, 16, 4, 4)],
        compiler_params=pltpu.CompilerParams(
            collective_id=0, has_side_effects=True, vmem_limit_bytes=60 << 20
        ),
        cost_estimate=pl.CostEstimate(flops=8_000_000_000, bytes_accessed=4_000_000, transcendentals=8_400_000),
    )(perm, slot_of, turn, queries, key_states, value_states, outputs, out_grad)


def solution(mesh):
    rows = P(("dp", "seq"), None)
    return jax.shard_map(
        per_device,
        mesh=mesh,
        in_specs=(rows, rows, rows, rows, rows, P("dp"), P()),
        out_specs=(rows, rows, rows),
        check_vma=False,
    )
```

time: 362 us -> 85.3 us (0.24)
  waiting for transfers between devices: 181 us -> 0 us
  matrix products: 81.7 us -> 0 us
  Pallas kernels: 0 us -> 76.6 us
  starting transfers between devices: 32.7 us -> 0 us
  local copies, waits for them, and re-layouts: 29.9 us -> 4.31 us
  other arithmetic: 17.9 us -> 1.54 us
  between operations: 15.6 us -> 1.34 us
    all_to_all x6 -> x0, waiting for transfers between devices: 129 us -> none  [the longest x1 24.2 us: per_device(): lax.all_to_all(out_grad, 'seq', split_axis=1, concat_axis=0, tiled=True)]
    dot_general x62 -> x0, matrix products: 81.7 us -> none  [the longest x10 30.1 us: gradient(): lax.dot_general(weights_half, grad_rows, contract_first, preferred_elemen...]
    pallas_call x0 -> x1, Pallas kernels: none -> 76.6 us  [per_device(): pl.pallas_call(kernel, out_shape=(shape((128, 3072), BF16), shape((128, 3...]
    all_gather x2 -> x0, waiting for transfers between devices: 51.9 us -> none  [the longest x1 51.9 us: per_device(): lax.all_gather(value_states, 'seq', axis=0, tiled=True)]
    all_to_all x6 -> x0, starting transfers between devices: 32.6 us -> none  [the longest x1 10.2 us: per_device(): lax.all_to_all(query_rot, 'seq', split_axis=1, concat_axis=0, tiled=True)]
    dynamic_slice x11 -> x0, local copies, waits for them, and re-layouts: 11.7 us -> none  [the longest x4 4.25 us: outer(): grad_rows = lax.dynamic_slice_in_dim(grad_head, query_start, block_size, 0)]
    reduce_sum x11 -> x2, other arithmetic: 11.1 us -> 0.78 us  [the longest x1 0.6 us: per_device(): jnp.sum(jnp.where(slot_of[:, None] == ids[None, :], ids[:, None], 0), axi...]
    unnamed x20 -> x11, local copies, waits for them, and re-layouts: 11.9 us -> 4.31 us
  transfers between devices with their start and end apart: 8 -> 0, of which waited for: 7 -> 0; matrix products, arithmetic and copies ran while one was open for 5% -> 0% of each run, Pallas kernels for 0% -> 0%
where the time goes in v2:
time: 85.3 us; the launch traced here: 83.8 us
  Pallas kernels  76.6 us (90%)
  local copies, waits for them, and re-layouts  4.31 us (5%)
  other arithmetic  1.54 us (2%)
  between operations  1.34 us (2%)
    pallas_call x1, Pallas kernels, per_device(): pl.pallas_call(kernel, out_shape=(shape((128, 3072), BF16), shape((128, 3...  76.6 us
    unnamed x11, local copies, waits for them, and re-layouts  4.31 us

profile of v2, /device:TPU:1, one launch (start us, length us, event | category | flops | bytes accessed | tf_op | source)
XLA Modules:
  0.0 83.8 jit_solution(8231358158699744268)
XLA Ops:
  1.3 0.0 copy-start.2
  1.3 0.6 copy-done.2
  1.9 0.2 convert_reduce_fusion
  2.1 0.0 copy-start.3
  2.1 0.6 select_reduce_fusion.perm
  2.7 0.0 copy-done.3
  2.7 0.1 multiply_cosine_fusion
  2.9 0.6 pad_maximum_fusion.turn
  3.5 76.6 %shard_map.94 = (bf16[128,3072]{1,0:T(8,128)(2,1)}, bf16[128,384]{1,0:T(8,128)(2,1)}, bf16[128,384]{1,0:T(8,128)(2,1)}) custom-call(s32[32]{0:T(128)} %select_reduce_fusion.perm, s32[32]{0:T(128)} %copy-done.3, f32[2,24,128]{2,1,0:T(8,128)} %pad_maximum_fusion.turn, bf16[128,3072]{1,0:T(8,128)(2,1)} %q_hbm.1, bf16[128,384]{1,0:T(8,128)(2,1)} %k_hbm.1, ...), custom_call_target="tpu_custom_call" | custom-call | flops 8000000000 | bytes 4000000 | tf_op jit(solution)/shard_map/pallas_call | solution.py:487
  80.1 0.0 copy-start.1
  80.1 2.1 %copy.14 = bf16[128,3072]{1,0:T(8,128)(2,1)} copy(bf16[128,3072]{1,0:T(8,128)(2,1)} %get-tuple-element.11) | data formatting | bytes 1572864
  82.2 0.0 copy-done.1
  82.2 0.0 copy-start
  82.2 0.6 copy.15
  82.9 0.3 copy-done
  83.1 0.6 copy.16
  (4 shorter events, 0.0 us)
Async XLA Ops:
  1.3 0.7 copy-start.2
  2.1 0.6 copy-start.3
  80.1 2.1 %copy-start.1 = (bf16[128,384]{1,0:T(8,128)(2,1)S(1)}, bf16[128,384]{1,0:T(8,128)(2,1)}, u32[]{:S(2)}) copy-start(bf16[128,384]{1,0:T(8,128)(2,1)} %get-tuple-element.12) | copy-start | bytes 294916
  82.2 0.9 %copy-start = (bf16[128,384]{1,0:T(8,128)(2,1)S(1)}, bf16[128,384]{1,0:T(8,128)(2,1)}, u32[]{:S(2)}) copy-start(bf16[128,384]{1,0:T(8,128)(2,1)} %get-tuple-element.13) | copy-start | bytes 294916

commit v3 on v2

v3 whole, which is shorter than its diff:
```python
import math

import jax
import jax.numpy as jnp
from jax import lax
from jax.experimental import pallas as pl
from jax.experimental.pallas import tpu as pltpu
from jax.sharding import PartitionSpec as P

HEADS = 32
GROUPS = 4
WIDTH = 96
ROT_DIM = 24
F32 = jnp.float32
BF16 = jnp.bfloat16
LN2 = math.log(2.0)
SCALE = WIDTH**-0.5
NT = (((1,), (1,)), ((), ()))
VM = pltpu.VMEM
GRAD_ROWS = 400


def split3(value):
    high = value.astype(BF16)
    rest = value - high.astype(F32)
    middle = rest.astype(BF16)
    low = (rest - middle.astype(F32)).astype(BF16)
    return high.astype(F32), middle.astype(F32), low.astype(F32)


def kernel(perm, slot_of, turn, q_hbm, k_hbm, v_hbm, o_hbm, g_hbm, dq_hbm, dk_hbm, dv_hbm,
           q_in, g_in, o_in, k_in, v_in, qt, gt, ot, kt, vt, dq_buf, dk_buf, dv_buf,
           ksrc, vsrc, kin, qsrc, gsrc, qin, gin,
           S0, S1, bias, Pm, D, QT, DO, Kn, Vn, KT, dKa, dVa, DQ, mrun, mfin, share,
           dq_src, dq_in, part, cin, zin, tot, fin,
           s_in, s_out, s_q, r_q, s_g, r_g, s_kx, r_kx, s_vx, r_vx, s_kz, r_kz, s_kc, r_kc,
           s_vz, r_vz, s_vc, r_vc, s_d, r_d, s_p, r_p, s_z, r_z, s_f, r_f):
    me = lax.axis_index("seq")
    x = me // 8
    z = (me // 2) % 4
    c = me % 2
    mine = x * 2 + c
    near = z + 1 - 2 * (z % 2)
    far = (z + 2) % 4
    cross = (near + 2) % 4
    mesh_id = pl.DeviceIdType.MESH
    mult = pl.multiple_of

    def at(px, pz, pc):
        return {"seq": px * 8 + pz * 2 + pc}

    def owner_at(p):
        return at(p // 2, z, p % 2)

    def remote(src, dst, send, recv, where):
        return pltpu.make_async_remote_copy(
            src_ref=src, dst_ref=dst, send_sem=send, recv_sem=recv,
            device_id=where, device_id_type=mesh_id,
        )

    def loads():
        pairs = ((k_hbm, k_in), (v_hbm, v_in), (q_hbm, q_in), (g_hbm, g_in), (o_hbm, o_in))
        return [pltpu.make_async_copy(a, b, s_in.at[i]) for i, (a, b) in enumerate(pairs)]

    incoming = loads()
    for copy in incoming:
        copy.start()
    barrier = pltpu.get_barrier_semaphore()
    for j in range(1, 8):
        pl.semaphore_signal(barrier, inc=1, device_id=owner_at(lax.rem(mine + j, 8)), device_id_type=mesh_id)
    for pz in (near, far, cross):
        pl.semaphore_signal(barrier, inc=1, device_id=at(x, pz, c), device_id_type=mesh_id)

    cosine = turn[0]
    sine = turn[1]

    def turned(rows):
        first = rows[0:ROT_DIM]
        swapped = jnp.concatenate([first[12:24], first[0:12]], axis=0)
        return jnp.concatenate([first * cosine + swapped * sine, rows[ROT_DIM:]], axis=0)

    def k_along_x(px, land):
        return remote(ksrc.at[px], kin.at[land, c, z], s_kx.at[px], r_kx.at[land], at(px, z, c))

    def v_along_x(px, land):
        return remote(vsrc.at[px], v_rows(land, c, z), s_vx.at[px], r_vx.at[land], at(px, z, c))

    def v_rows(px, pc, pz):
        return Vn.at[px, pl.ds(mult((pc * 4 + pz) * 128, 128), 128)]

    def k_along_z(px, block, pz):
        return remote(kin.at[px, c, block], kin.at[px, c, block], s_kz.at[px * 4 + pz],
                      r_kz.at[px * 4 + block], at(x, pz, c))

    def v_along_z(px, block, pz):
        return remote(v_rows(px, c, block), v_rows(px, c, block), s_vz.at[px * 4 + pz],
                      r_vz.at[px * 4 + block], at(x, pz, c))

    def k_to_core(px, land):
        return remote(kin.at[px, land], kin.at[px, land], s_kc.at[px], r_kc.at[px], at(x, z, 1 - c))

    def v_to_core(px, land):
        rows = Vn.at[px, pl.ds(mult(land * 512, 128), 512)]
        return remote(rows, rows, s_vc.at[px], r_vc.at[px], at(x, z, 1 - c))

    def q_move(p, land):
        return remote(qsrc.at[p], qin.at[land], s_q.at[p], r_q.at[land], owner_at(p))

    def g_move(p, land):
        return remote(gsrc.at[p], gin.at[land], s_g.at[p], r_g.at[land], owner_at(p))

    def dq_move(p, land):
        return remote(dq_src.at[p], dq_in.at[pl.ds(land * 4, 4)], s_d.at[p], r_d.at[land], owner_at(p))

    def part_move(px):
        return remote(part.at[px, 1 - c], cin.at[px], s_p.at[px], r_p.at[px], at(x, z, 1 - c))

    def sum_along_z(px, block, pz, way):
        return remote(part.at[px, c, block], zin.at[px, way], s_z.at[px * 3 + way], r_z.at[px * 3 + way], at(x, pz, c))

    def total_move(px, land):
        return remote(tot.at[px], fin.at[land], s_f.at[px], r_f.at[land], at(px, z, c))

    def over_x(action):
        for j in range(1, 4):
            action(lax.rem(x + j, 4))

    others = (far, cross, near)

    incoming[0].wait()
    for j in range(3):
        lanes = slice(j * 128, j * 128 + 128)
        kt[lanes, :] = k_in[:, lanes].T
    for g in range(GROUPS):
        ksrc[g] = turned(kt[g * WIDTH : (g + 1) * WIDTH, :].astype(F32)).astype(BF16)
    pl.semaphore_wait(barrier, 10)
    over_x(lambda px: k_along_x(px, x).start())
    kin[x, c, z] = ksrc[x]
    incoming[1].wait()
    value_tail = (lax.broadcasted_iota(jnp.int32, (128, 32), 1) < 3).astype(BF16)
    for g in range(GROUPS):
        vsrc[g] = jnp.concatenate([v_in[:, g * WIDTH : (g + 1) * WIDTH], value_tail], axis=1)
    over_x(lambda px: v_along_x(px, x).start())
    Vn[x, pl.ds(mult((c * 4 + z) * 128, 128), 128), :] = vsrc[x]

    incoming[2].wait()

    def flip_q(j, _):
        rows = q_in[:, pl.ds(mult(j * 384, 128), 384)].T
        for i in range(4):
            qt[j * 4 + i] = rows[i * WIDTH : (i + 1) * WIDTH]
        return 0

    lax.fori_loop(0, 8, flip_q, 0)

    def send_q(j, _):
        p = lax.rem(mine + j, 8)
        for i in range(4):
            rows = qt[perm[p * 4 + i]]
            qsrc[p, i * WIDTH : (i + 1) * WIDTH, :] = (turned(rows.astype(F32)) * (SCALE / LN2)).astype(BF16)

        @pl.when(j < 8)
        def _():
            q_move(p, mine).start()

        return 0

    lax.fori_loop(1, 9, send_q, 0)
    qin[mine] = qsrc[mine]

    def spread_k(px, _):
        @pl.when(px != x)
        def _():
            k_along_x(px, px).wait_recv()

        for pz in others:
            k_along_z(px, z, pz).start()
        return 0

    lax.fori_loop(0, 4, spread_k, 0)

    incoming[3].wait()
    incoming[4].wait()

    def flip_g(j, _):
        lanes = pl.ds(mult(j * 384, 128), 384)
        grads = g_in[:, lanes].T
        outs = o_in[:, lanes].T
        for i in range(4):
            gt[j * 4 + i] = grads[i * WIDTH : (i + 1) * WIDTH]
            ot[j * 4 + i] = outs[i * WIDTH : (i + 1) * WIDTH]
        return 0

    lax.fori_loop(0, 8, flip_g, 0)

    def make_g(j, _):
        p = lax.rem(mine + j, 8)
        deltas = []
        for i in range(4):
            head = perm[p * 4 + i]
            grad = gt[head]
            gsrc[p, i * WIDTH : (i + 1) * WIDTH, :] = grad
            deltas.append(jnp.sum(grad.astype(F32) * ot[head].astype(F32), axis=0, keepdims=True))
        high, middle, low = split3(jnp.concatenate(deltas, axis=0))
        gsrc[p, 384:400, :] = jnp.concatenate(
            [high, middle, low, jnp.zeros((4, 128), F32)], axis=0
        ).astype(BF16)
        return 0

    lax.fori_loop(1, 9, make_g, 0)
    gin[mine] = gsrc[mine]


    def spread_v(px):
        for pz in others:
            v_along_z(px, z, pz).start()

    def send_g(j, _):
        g_move(lax.rem(mine + j, 8), mine).start()
        return 0

    def make_bias(i, _):
        rows = pl.ds(mult(i * 128, 128), 128)
        key_id = lax.broadcasted_iota(jnp.int32, (128, 256), 0) + (i % 4 - z) * 256 + (i // 4) * 128
        bias[0, rows, :] = jnp.zeros((128, 256), F32)
        bias[1, rows, :] = jnp.where(key_id <= lax.broadcasted_iota(jnp.int32, (128, 256), 1), 0.0, -1e30)
        return 0

    lax.fori_loop(0, 8, make_bias, 0)

    def clear(i, _):
        dKa[i] = jnp.zeros((96, 1024), F32)
        dVa[i] = jnp.zeros((96, 1024), F32)
        DQ[i] = jnp.zeros((96, 1024), F32)
        return 0

    lax.fori_loop(0, 4, clear, 0)
    QT[:, 96:128, :] = jnp.zeros((4, 32, 1024), BF16)

    def share_k(px):
        for pz in others:
            k_along_z(px, pz, pz).wait_recv()
        k_to_core(px, c).start()

    heads = [slice(h * 256, h * 256 + 256) for h in range(4)]
    zero_rows = jnp.zeros((32, 128), BF16)

    def ready_k(px):
        k_to_core(px, 1 - c).wait_recv()
        for b in range(8):
            lanes = slice(b * 128, b * 128 + 128)
            keys = kin[px, b // 4, b % 4]
            KT[px, :, lanes] = keys
            Kn[px, lanes, :] = jnp.concatenate([keys, zero_rows], 0).T

    def ready_q(qx):
        for half in range(2):
            p = qx * 2 + half

            @pl.when(p != mine)
            def _():
                q_move(p, p).wait_recv()

        for h in range(4):
            for half in range(2):
                start = h * 256 + half * 128
                QT[qx, 0:96, start : start + 128] = qin[qx * 2 + half, h * 96 : h * 96 + 96, :]

    def place(i):
        qx = jnp.minimum(i, 1) + jnp.clip(i - 2, 0, 1) + jnp.clip(i - 5, 0, 1)
        return qx, i - qx * (qx + 1) // 2

    def weigh(i, h, held, top, before, total):
        qx, px = place(i)
        p = jnp.exp2(held[:, heads[h]] - top)
        Pm[i, :, heads[h]] = p.astype(BF16)
        mrun[i, :, heads[h]] = top
        kept = jnp.where(px == 0, 0.0, total * jnp.exp2(before - top))
        return kept + jnp.sum(p.reshape(128, 8, 256), axis=0)

    def settle(i, state):
        qx, px = place(i)
        for h in range(4):
            mfin[qx, :, heads[h]] = state[h]
            share[qx, :, heads[h]] = 1.0 / jnp.sum(state[4 + h], axis=0, keepdims=True)

    def score_pair(t, state):
        @pl.when(t == 0)
        def _():
            share_k(0)
            ready_q(0)
            ready_q(1)
            ready_k(0)
            lax.fori_loop(1, 8, send_g, 0)

        @pl.when(t == 1)
        def _():
            share_k(1)
            share_k(2)
            ready_q(2)
            ready_k(1)
            over_x(lambda px: v_along_x(px, px).wait_recv())
            spread_v(3)

        @pl.when(t == 2)
        def _():
            share_k(3)
            ready_k(2)
            spread_v(2)

        @pl.when(t == 3)
        def _():
            ready_q(3)
            spread_v(1)

        @pl.when(t == 4)
        def _():
            ready_k(3)
            spread_v(0)
            share_v(3)

        top, total, before = list(state[:4]), list(state[4:8]), list(state[8:12])
        for u in range(2):
            i = 2 * t + u
            qx, px = place(i)
            filled, held = (S0, S1) if u == 0 else (S1, S0)
            diagonal = jnp.where(qx == px, 1, 0)
            new_top = [None] * 4
            last = jnp.maximum(i - 1, 0)
            for h in range(4):
                s = jnp.dot(Kn[px], QT[qx, :, heads[h]], preferred_element_type=F32) + bias[diagonal]
                filled[:, heads[h]] = s
                high = jnp.max(jnp.max(s.reshape(128, 8, 256), axis=0), axis=0, keepdims=True)
                new_top[h] = jnp.maximum(jnp.where(px == 0, -1e30, top[h]), high)
                total[h] = weigh(last, h, held, top[h], before[h], total[h])
            settle(last, top + total)
            before, top = top, new_top
        return tuple(top) + tuple(total) + tuple(before)

    def share_v(px):
        for pz in others:
            v_along_z(px, pz, pz).wait_recv()
        v_to_core(px, c).start()

    S1[...] = jnp.zeros((1024, 1024), F32)
    low = tuple(jnp.full((1, 256), -1e30, F32) for _ in range(4))
    none = tuple(jnp.zeros((8, 256), F32) for _ in range(4))
    zeros = tuple(jnp.zeros((1, 256), F32) for _ in range(4))
    state = lax.fori_loop(0, 5, score_pair, zeros + none + zeros)
    total = [weigh(9, h, S1, state[h], state[8 + h], state[4 + h]) for h in range(4)]
    settle(9, list(state[:4]) + total)

    row_id = lax.broadcasted_iota(jnp.int32, (32, 128), 0)

    def reduce_cores(px):
        part_move(px).wait()

        def add(b, _):
            part[px, c, b] = (part[px, c, b].astype(F32) + cin[px, b].astype(F32)).astype(BF16)
            return 0

        lax.fori_loop(0, 4, add, 0)
        sum_along_z(px, cross, near, 1).start()
        sum_along_z(px, near, near, 0).start()

    def reduce_near(px):
        sum_along_z(px, cross, near, 1).wait_recv()
        sum_along_z(px, cross, near, 1).wait_send()
        part[px, c, far] = (part[px, c, far].astype(F32) + zin[px, 1].astype(F32)).astype(BF16)
        sum_along_z(px, far, far, 2).start()

    def reduce_far(px):
        sum_along_z(px, near, near, 0).wait_recv()
        sum_along_z(px, far, far, 2).wait_recv()
        tot[px] = (part[px, c, z].astype(F32) + zin[px, 0].astype(F32) + zin[px, 2].astype(F32)).astype(BF16)

        @pl.when(px != x)
        def _():
            total_move(px, x).start()

        @pl.when(px == x)
        def _():
            fin[x] = tot[px]

    def gradients(n, _):
        group, rank = place(n)
        px = 3 - group
        turn_round = jnp.clip(group - 2, 0, 1)
        qx = turn_round * lax.rem(x + 1 + rank, 4) + (1 - turn_round) * (3 - rank)

        for number, column in ((0, 3), (1, 2), (3, 1), (6, 0)):
            @pl.when(n == number)
            def _():
                for p in (column * 2, column * 2 + 1):
                    @pl.when(p != mine)
                    def _():
                        g_move(p, p).wait_recv()

                if column > 0:
                    share_v(column - 1)
                v_to_core(column, 1 - c).wait_recv()

        block = qx * (qx + 1) // 2 + px
        factor = jnp.exp2(mrun[block] - mfin[qx]) * share[qx]
        for h in range(4):
            for half in range(2):
                start = h * 256 + half * 128
                scale = factor[:, start : start + 128]
                grad = gin[qx * 2 + half, h * 96 : h * 96 + 96, :]
                DO[0:96, start : start + 128] = (grad.astype(F32) * scale).astype(BF16)
                d = gin[qx * 2 + half, 384:400, :].astype(F32)
                d = -(d[h : h + 1] + d[4 + h : 5 + h] + d[8 + h : 9 + h]) * scale
                high, middle, low = split3(d)
                DO[96:128, start : start + 128] = jnp.where(
                    row_id == 0, high, jnp.where(row_id == 1, middle, jnp.where(row_id == 2, low, 0.0))
                ).astype(BF16)
        for h in range(4):
            for r in range(4):
                rows = slice(r * 256, r * 256 + 256)
                dp = jnp.dot(Vn[px, rows, :], DO[:, heads[h]], preferred_element_type=F32)
                D[rows, heads[h]] = (Pm[block, rows, heads[h]].astype(F32) * dp).astype(BF16)
            dVa[px] += lax.dot_general(DO[0:96, heads[h]], Pm[block, :, heads[h]], NT,
                                       preferred_element_type=F32)
            dKa[px] += lax.dot_general(QT[qx, 0:96, heads[h]], D[:, heads[h]], NT, preferred_element_type=F32)
            DQ[qx, :, heads[h]] += jnp.dot(KT[px], D[:, heads[h]], preferred_element_type=F32)

        @pl.when(px == 0)
        def _():
            for half in range(2):
                p = qx * 2 + half
                for h in range(4):
                    start = h * 256 + half * 128
                    dq_src[p, h] = (DQ[qx, :, start : start + 128] * SCALE).astype(BF16)

                @pl.when(p != mine)
                def _():
                    dq_move(p, mine).start()

        @pl.when(rank == group)
        def _():
            for b in range(8):
                lanes = slice(b * 128, b * 128 + 128)
                part[px, b // 4, b % 4, 0:96, :] = (dKa[px, :, lanes] * LN2).astype(BF16)
                part[px, b // 4, b % 4, 96:192, :] = dVa[px, :, lanes].astype(BF16)
            part_move(px).start()

        def after(number, *steps):
            @pl.when(n == number)
            def _():
                for step, column in steps:
                    step(column)

        after(1, (reduce_cores, 3))
        after(3, (reduce_cores, 2), (reduce_near, 3))
        after(5, (reduce_near, 2), (reduce_far, 3))
        after(6, (reduce_cores, 1))
        after(7, (reduce_far, 2))
        after(8, (reduce_near, 1))
        return 0

    lax.fori_loop(0, 10, gradients, 0)
    reduce_cores(0)
    reduce_far(1)
    reduce_near(0)

    dq_in[pl.ds(mine * 4, 4)] = dq_src[mine]

    def arrive_dq(j, _):
        p = lax.rem(mine + j, 8)
        dq_move(p, p).wait_recv()
        return 0

    lax.fori_loop(1, 8, arrive_dq, 0)
    def flip_back(j, _):
        rows = jnp.concatenate([dq_in[slot_of[j * 4 + i]] for i in range(4)], axis=0)
        dq_buf[:, pl.ds(mult(j * 384, 128), 384)] = rows.T
        return 0

    lax.fori_loop(0, 8, flip_back, 0)
    outgoing = [pltpu.make_async_copy(dq_buf, dq_hbm, s_out.at[0])]
    outgoing[0].start()
    reduce_far(0)
    over_x(lambda px: total_move(px, px).wait_recv())
    for g in range(GROUPS):
        kt[g * WIDTH : (g + 1) * WIDTH, :] = fin[g, 0:96, :]
        vt[g * WIDTH : (g + 1) * WIDTH, :] = fin[g, 96:192, :]
    for j in range(3):
        lanes = slice(j * 128, j * 128 + 128)
        dk_buf[:, lanes] = kt[lanes, :].T
        dv_buf[:, lanes] = vt[lanes, :].T
    outgoing.append(pltpu.make_async_copy(dk_buf, dk_hbm, s_out.at[1]))
    outgoing.append(pltpu.make_async_copy(dv_buf, dv_hbm, s_out.at[2]))
    outgoing[1].start()
    outgoing[2].start()

    def sent(p):
        q_move(p, mine).wait_send()
        g_move(p, mine).wait_send()
        dq_move(p, mine).wait_send()

    def sent_all(j, _):
        sent(lax.rem(mine + j, 8))
        return 0

    lax.fori_loop(1, 8, sent_all, 0)

    def sent_x(px):
        k_along_x(px, x).wait_send()
        v_along_x(px, x).wait_send()
        total_move(px, x).wait_send()

    over_x(sent_x)

    def sent_z(px, _):
        for pz in others:
            k_along_z(px, z, pz).wait_send()
            v_along_z(px, z, pz).wait_send()
        sum_along_z(px, near, near, 0).wait_send()
        sum_along_z(px, far, far, 2).wait_send()
        k_to_core(px, c).wait_send()
        v_to_core(px, c).wait_send()
        return 0

    lax.fori_loop(0, 4, sent_z, 0)
    for copy in outgoing:
        copy.wait()


def per_device(queries, key_states, value_states, outputs, out_grad, window_start, head_group):
    in_vmem = pl.BlockSpec(memory_space=VM)
    in_smem = pl.BlockSpec(memory_space=pltpu.SMEM)
    anywhere = pl.BlockSpec(memory_space=pl.ANY)
    shape = jax.ShapeDtypeStruct
    me = lax.axis_index("seq")
    position = (window_start[0] + me * 128 + jnp.arange(128, dtype=jnp.int32)).astype(F32)
    half = ROT_DIM // 2
    frequency = 10000.0 ** (-2.0 * jnp.arange(half, dtype=F32) / ROT_DIM)
    angles = position[None, :] * frequency[:, None]
    cosine, sine = jnp.cos(angles), jnp.sin(angles)
    turn = jnp.stack([jnp.concatenate([cosine, cosine], 0), jnp.concatenate([-sine, sine], 0)])
    ids = jnp.arange(HEADS, dtype=jnp.int32)
    same = (head_group[:, None] == head_group[None, :]) & (ids[None, :] < ids[:, None])
    slot_of = head_group * 8 + jnp.sum(same.astype(jnp.int32), axis=1)
    perm = jnp.sum(jnp.where(slot_of[:, None] == ids[None, :], ids[:, None], 0), axis=0)
    dma = pltpu.SemaphoreType.DMA
    wide = VM((128, 3072), BF16)
    tall = VM((HEADS, WIDTH, 128), BF16)
    small = VM((128, 384), BF16)
    small_t = VM((384, 128), BF16)
    return pl.pallas_call(
        kernel,
        out_shape=(shape((128, 3072), BF16), shape((128, 384), BF16), shape((128, 384), BF16)),
        in_specs=[in_smem, in_smem, in_vmem] + [anywhere] * 5,
        out_specs=(anywhere, anywhere, anywhere),
        scratch_shapes=[
            wide, wide, wide, small, small, tall, tall, tall, small_t, small_t, wide, small, small,
            VM((4, 96, 128), BF16), VM((4, 128, 128), BF16),
            VM((4, 2, 4, 96, 128), BF16),
            VM((8, 384, 128), BF16), VM((8, GRAD_ROWS, 128), BF16),
            VM((8, 384, 128), BF16), VM((8, GRAD_ROWS, 128), BF16),
            VM((1024, 1024), F32), VM((1024, 1024), F32), VM((2, 1024, 256), F32), VM((10, 1024, 1024), BF16), VM((1024, 1024), BF16),
            VM((4, 128, 1024), BF16), VM((128, 1024), BF16),
            VM((4, 1024, 128), BF16), VM((4, 1024, 128), BF16), VM((4, 96, 1024), BF16),
            VM((4, 96, 1024), F32), VM((4, 96, 1024), F32), VM((4, 96, 1024), F32),
            VM((10, 1, 1024), F32), VM((4, 1, 1024), F32), VM((4, 1, 1024), F32),
            VM((8, 4, 96, 128), BF16), VM((32, 96, 128), BF16),
            VM((4, 2, 4, 192, 128), BF16), VM((4, 4, 192, 128), BF16), VM((4, 3, 192, 128), BF16),
            VM((4, 192, 128), BF16), VM((4, 192, 128), BF16),
        ]
        + [dma((n,)) for n in (5, 3, 8, 8, 8, 8, 4, 4, 4, 4, 16, 16, 4, 4, 16, 16, 4, 4, 8, 8, 4, 4, 12, 12, 4, 4)],
        compiler_params=pltpu.CompilerParams(
            collective_id=0, has_side_effects=True, vmem_limit_bytes=60 << 20
        ),
        cost_estimate=pl.CostEstimate(flops=8_000_000_000, bytes_accessed=4_000_000, transcendentals=8_400_000),
    )(perm, slot_of, turn, queries, key_states, value_states, outputs, out_grad)


def solution(mesh):
    rows = P(("dp", "seq"), None)
    return jax.shard_map(
        per_device,
        mesh=mesh,
        in_specs=(rows, rows, rows, rows, rows, P("dp"), P()),
        out_specs=(rows, rows, rows),
        check_vma=False,
    )
```

time: 85.3 us -> 80.2 us (0.940); the launches traced: 83.8 us -> 80 us
  Pallas kernels: 76.6 us -> 72.8 us
    pallas_call x1, Pallas kernels: 76.6 us -> 72.8 us  [per_device(): pl.pallas_call(kernel, out_shape=(shape((128, 3072), BF16), shape((128, 3...]
where the time goes in v3:
time: 80.2 us; the launch traced here: 80 us
  Pallas kernels  72.8 us (91%)
  local copies, waits for them, and re-layouts  4.31 us (5%)
  other arithmetic  1.54 us (2%)
  between operations  1.34 us (2%)
    pallas_call x1, Pallas kernels, per_device(): pl.pallas_call(kernel, out_shape=(shape((128, 3072), BF16), shape((128, 3...  72.8 us
    unnamed x11, local copies, waits for them, and re-layouts  4.31 us

profile of v3, /device:TPU:1, one launch (start us, length us, event | category | flops | bytes accessed | tf_op | source)
XLA Modules:
  0.0 80.0 jit_solution(6333547852646027833)
XLA Ops:
  1.3 0.0 copy-start.2
  1.3 0.6 copy-done.2
  1.9 0.2 convert_reduce_fusion
  2.1 0.0 copy-start.3
  2.1 0.6 select_reduce_fusion.perm
  2.7 0.0 copy-done.3
  2.7 0.1 multiply_cosine_fusion
  2.9 0.6 pad_maximum_fusion.turn
  3.5 72.8 %shard_map.94 = (bf16[128,3072]{1,0:T(8,128)(2,1)}, bf16[128,384]{1,0:T(8,128)(2,1)}, bf16[128,384]{1,0:T(8,128)(2,1)}) custom-call(s32[32]{0:T(128)} %select_reduce_fusion.perm, s32[32]{0:T(128)} %copy-done.3, f32[2,24,128]{2,1,0:T(8,128)} %pad_maximum_fusion.turn, bf16[128,3072]{1,0:T(8,128)(2,1)} %q_hbm.1, bf16[128,384]{1,0:T(8,128)(2,1)} %k_hbm.1, ...), custom_call_target="tpu_custom_call" | custom-call | flops 8000000000 | bytes 4000000 | tf_op jit(solution)/shard_map/pallas_call | solution.py:550
  76.3 0.0 copy-start.1
  76.3 2.1 %copy.14 = bf16[128,3072]{1,0:T(8,128)(2,1)} copy(bf16[128,3072]{1,0:T(8,128)(2,1)} %get-tuple-element.11) | data formatting | bytes 1572864
  78.4 0.0 copy-done.1
  78.4 0.0 copy-start
  78.4 0.6 copy.15
  79.0 0.3 copy-done
  79.3 0.6 copy.16
  (4 shorter events, 0.0 us)
Async XLA Ops:
  1.3 0.7 copy-start.2
  2.1 0.6 copy-start.3
  76.3 2.1 %copy-start.1 = (bf16[128,384]{1,0:T(8,128)(2,1)S(1)}, bf16[128,384]{1,0:T(8,128)(2,1)}, u32[]{:S(2)}) copy-start(bf16[128,384]{1,0:T(8,128)(2,1)} %get-tuple-element.12) | copy-start | bytes 294916
  78.4 0.9 %copy-start = (bf16[128,384]{1,0:T(8,128)(2,1)S(1)}, bf16[128,384]{1,0:T(8,128)(2,1)}, u32[]{:S(2)}) copy-start(bf16[128,384]{1,0:T(8,128)(2,1)} %get-tuple-element.13) | copy-start | bytes 294916

commit v4 on v3

--- a/solution.py
+++ b/solution.py
@@ -29,7 +29,7 @@
 
 
 def kernel(perm, slot_of, turn, q_hbm, k_hbm, v_hbm, o_hbm, g_hbm, dq_hbm, dk_hbm, dv_hbm,
-           q_in, g_in, o_in, k_in, v_in, qt, gt, ot, kt, vt, dq_buf, dk_buf, dv_buf,
+           q_in, g_in, o_in, k_in, v_in, qt, gt, ot, kt, vt, dk_buf, dv_buf,
            ksrc, vsrc, kin, qsrc, gsrc, qin, gin,
            S0, S1, bias, Pm, D, QT, DO, Kn, Vn, KT, dKa, dVa, DQ, mrun, mfin, share,
            dq_src, dq_in, part, cin, zin, tot, fin,
@@ -360,7 +360,16 @@
             return 0
 
         lax.fori_loop(0, 4, add, 0)
+
+    def send_two_hops(px):
+        reduce_cores(px)
         sum_along_z(px, cross, near, 1).start()
+        sum_along_z(px, near, near, 0).start()
+
+    def send_one_hop(px):
+        reduce_cores(px)
+        sum_along_z(px, far, far, 2).start()
+        sum_along_z(px, cross, cross, 1).start()
         sum_along_z(px, near, near, 0).start()
 
     def reduce_near(px):
@@ -369,10 +378,14 @@
         part[px, c, far] = (part[px, c, far].astype(F32) + zin[px, 1].astype(F32)).astype(BF16)
         sum_along_z(px, far, far, 2).start()
 
-    def reduce_far(px):
+    def reduce_far(px, one_hop=False):
         sum_along_z(px, near, near, 0).wait_recv()
         sum_along_z(px, far, far, 2).wait_recv()
-        tot[px] = (part[px, c, z].astype(F32) + zin[px, 0].astype(F32) + zin[px, 2].astype(F32)).astype(BF16)
+        total = part[px, c, z].astype(F32) + zin[px, 0].astype(F32) + zin[px, 2].astype(F32)
+        if one_hop:
+            sum_along_z(px, cross, cross, 1).wait_recv()
+            total = total + zin[px, 1].astype(F32)
+        tot[px] = total.astype(BF16)
 
         @pl.when(px != x)
         def _():
@@ -382,7 +395,7 @@
         def _():
             fin[x] = tot[px]
 
-    def gradients(n, _):
+    def gradients(n, _, late=False):
         group, rank = place(n)
         px = 3 - group
         turn_round = jnp.clip(group - 2, 0, 1)
@@ -401,6 +414,7 @@
                 v_to_core(column, 1 - c).wait_recv()
 
         block = qx * (qx + 1) // 2 + px
+        held = D.at[rank] if late else D.at[0]
         factor = jnp.exp2(mrun[block] - mfin[qx]) * share[qx]
         for h in range(4):
             for half in range(2):
@@ -418,23 +432,12 @@
             for r in range(4):
                 rows = slice(r * 256, r * 256 + 256)
                 dp = jnp.dot(Vn[px, rows, :], DO[:, heads[h]], preferred_element_type=F32)
-                D[rows, heads[h]] = (Pm[block, rows, heads[h]].astype(F32) * dp).astype(BF16)
+                held[rows, heads[h]] = (Pm[block, rows, heads[h]].astype(F32) * dp).astype(BF16)
             dVa[px] += lax.dot_general(DO[0:96, heads[h]], Pm[block, :, heads[h]], NT,
                                        preferred_element_type=F32)
-            dKa[px] += lax.dot_general(QT[qx, 0:96, heads[h]], D[:, heads[h]], NT, preferred_element_type=F32)
-            DQ[qx, :, heads[h]] += jnp.dot(KT[px], D[:, heads[h]], preferred_element_type=F32)
-
-        @pl.when(px == 0)
-        def _():
-            for half in range(2):
-                p = qx * 2 + half
-                for h in range(4):
-                    start = h * 256 + half * 128
-                    dq_src[p, h] = (DQ[qx, :, start : start + 128] * SCALE).astype(BF16)
-
-                @pl.when(p != mine)
-                def _():
-                    dq_move(p, mine).start()
+            dKa[px] += lax.dot_general(QT[qx, 0:96, heads[h]], held[:, heads[h]], NT, preferred_element_type=F32)
+            if not late:
+                DQ[qx, :, heads[h]] += jnp.dot(KT[px], held[:, heads[h]], preferred_element_type=F32)
 
         @pl.when(rank == group)
         def _():
@@ -450,18 +453,37 @@
                 for step, column in steps:
                     step(column)
 
-        after(1, (reduce_cores, 3))
-        after(3, (reduce_cores, 2), (reduce_near, 3))
+        after(1, (send_two_hops, 3))
+        after(3, (send_two_hops, 2), (reduce_near, 3))
         after(5, (reduce_near, 2), (reduce_far, 3))
-        after(6, (reduce_cores, 1))
+        after(6, (send_two_hops, 1))
         after(7, (reduce_far, 2))
         after(8, (reduce_near, 1))
         return 0
 
-    lax.fori_loop(0, 10, gradients, 0)
-    reduce_cores(0)
+    lax.fori_loop(0, 6, gradients, 0)
+    lax.fori_loop(6, 10, lambda n, _: gradients(n, _, late=True), 0)
+
+    def late_queries(rank, _):
+        qx = lax.rem(x + 1 + rank, 4)
+        for h in range(4):
+            grad = DQ[qx, :, heads[h]] + jnp.dot(KT[0], D[rank, :, heads[h]], preferred_element_type=F32)
+            for half in range(2):
+                dq_src[qx * 2 + half, h] = (grad[:, half * 128 : half * 128 + 128] * SCALE).astype(BF16)
+        for half in range(2):
+            p = qx * 2 + half
+
+            @pl.when(p != mine)
+            def _():
+                dq_move(p, mine).start()
+
+        return 0
+
+    lax.fori_loop(0, 3, late_queries, 0)
+    send_one_hop(0)
+    late_queries(3, 0)
     reduce_far(1)
-    reduce_near(0)
+    reduce_far(0, one_hop=True)
 
     dq_in[pl.ds(mine * 4, 4)] = dq_src[mine]
 
@@ -473,13 +495,13 @@
     lax.fori_loop(1, 8, arrive_dq, 0)
     def flip_back(j, _):
         rows = jnp.concatenate([dq_in[slot_of[j * 4 + i]] for i in range(4)], axis=0)
-        dq_buf[:, pl.ds(mult(j * 384, 128), 384)] = rows.T
+        q_in[:, pl.ds(mult(j * 384, 128), 384)] = rows.T
         return 0
 
     lax.fori_loop(0, 8, flip_back, 0)
-    outgoing = [pltpu.make_async_copy(dq_buf, dq_hbm, s_out.at[0])]
+    outgoing = [pltpu.make_async_copy(q_in, dq_hbm, s_out.at[0])]
     outgoing[0].start()
-    reduce_far(0)
+    sum_along_z(0, cross, cross, 1).wait_send()
     over_x(lambda px: total_move(px, px).wait_recv())
     for g in range(GROUPS):
         kt[g * WIDTH : (g + 1) * WIDTH, :] = fin[g, 0:96, :]
@@ -553,12 +575,12 @@
         in_specs=[in_smem, in_smem, in_vmem] + [anywhere] * 5,
         out_specs=(anywhere, anywhere, anywhere),
         scratch_shapes=[
-            wide, wide, wide, small, small, tall, tall, tall, small_t, small_t, wide, small, small,
+            wide, wide, wide, small, small, tall, tall, tall, small_t, small_t, small, small,
             VM((4, 96, 128), BF16), VM((4, 128, 128), BF16),
             VM((4, 2, 4, 96, 128), BF16),
             VM((8, 384, 128), BF16), VM((8, GRAD_ROWS, 128), BF16),
             VM((8, 384, 128), BF16), VM((8, GRAD_ROWS, 128), BF16),
-            VM((1024, 1024), F32), VM((1024, 1024), F32), VM((2, 1024, 256), F32), VM((10, 1024, 1024), BF16), VM((1024, 1024), BF16),
+            VM((1024, 1024), F32), VM((1024, 1024), F32), VM((2, 1024, 256), F32), VM((10, 1024, 1024), BF16), VM((4, 1024, 1024), BF16),
             VM((4, 128, 1024), BF16), VM((128, 1024), BF16),
             VM((4, 1024, 128), BF16), VM((4, 1024, 128), BF16), VM((4, 96, 1024), BF16),
             VM((4, 96, 1024), F32), VM((4, 96, 1024), F32), VM((4, 96, 1024), F32),
@@ -569,7 +591,7 @@
         ]
         + [dma((n,)) for n in (5, 3, 8, 8, 8, 8, 4, 4, 4, 4, 16, 16, 4, 4, 16, 16, 4, 4, 8, 8, 4, 4, 12, 12, 4, 4)],
         compiler_params=pltpu.CompilerParams(
-            collective_id=0, has_side_effects=True, vmem_limit_bytes=60 << 20
+            collective_id=0, has_side_effects=True, vmem_limit_bytes=62 << 20
         ),
         cost_estimate=pl.CostEstimate(flops=8_000_000_000, bytes_accessed=4_000_000, transcendentals=8_400_000),
     )(perm, slot_of, turn, queries, key_states, value_states, outputs, out_grad)

time: 80.2 us -> 78.7 us (0.981)
  Pallas kernels: 72.8 us -> 71.2 us
    pallas_call x1, Pallas kernels: 72.8 us -> 71.2 us  [per_device(): pl.pallas_call(kernel, out_shape=(shape((128, 3072), BF16), shape((128, 3...]
where the time goes in v4:
time: 78.7 us; the launch traced here: 78.4 us
  Pallas kernels  71.2 us (90%)
  local copies, waits for them, and re-layouts  4.31 us (5%)
  other arithmetic  1.54 us (2%)
  between operations  1.34 us (2%)
    pallas_call x1, Pallas kernels, per_device(): pl.pallas_call(kernel, out_shape=(shape((128, 3072), BF16), shape((128, 3...  71.2 us
    unnamed x11, local copies, waits for them, and re-layouts  4.31 us

profile of v4, /device:TPU:1, one launch (start us, length us, event | category | flops | bytes accessed | tf_op | source)
XLA Modules:
  0.0 78.4 jit_solution(9520031957678023064)
XLA Ops:
  1.3 0.0 copy-start.2
  1.3 0.6 copy-done.2
  1.9 0.2 convert_reduce_fusion
  2.1 0.0 copy-start.3
  2.1 0.6 select_reduce_fusion.perm
  2.7 0.0 copy-done.3
  2.7 0.1 multiply_cosine_fusion
  2.9 0.6 pad_maximum_fusion.turn
  3.5 71.2 %shard_map.94 = (bf16[128,3072]{1,0:T(8,128)(2,1)}, bf16[128,384]{1,0:T(8,128)(2,1)}, bf16[128,384]{1,0:T(8,128)(2,1)}) custom-call(s32[32]{0:T(128)} %select_reduce_fusion.perm, s32[32]{0:T(128)} %copy-done.3, f32[2,24,128]{2,1,0:T(8,128)} %pad_maximum_fusion.turn, bf16[128,3072]{1,0:T(8,128)(2,1)} %q_hbm.1, bf16[128,384]{1,0:T(8,128)(2,1)} %k_hbm.1, ...), custom_call_target="tpu_custom_call" | custom-call | flops 8000000000 | bytes 4000000 | tf_op jit(solution)/shard_map/pallas_call | solution.py:572
  74.7 0.0 copy-start.1
  74.8 2.1 %copy.14 = bf16[128,3072]{1,0:T(8,128)(2,1)} copy(bf16[128,3072]{1,0:T(8,128)(2,1)} %get-tuple-element.11) | data formatting | bytes 1572864
  76.9 0.0 copy-done.1
  76.9 0.0 copy-start
  76.9 0.6 copy.15
  77.5 0.3 copy-done
  77.8 0.6 copy.16
  (4 shorter events, 0.0 us)
Async XLA Ops:
  1.3 0.7 copy-start.2
  2.1 0.6 copy-start.3
  74.7 2.1 %copy-start.1 = (bf16[128,384]{1,0:T(8,128)(2,1)S(1)}, bf16[128,384]{1,0:T(8,128)(2,1)}, u32[]{:S(2)}) copy-start(bf16[128,384]{1,0:T(8,128)(2,1)} %get-tuple-element.12) | copy-start | bytes 294916
  76.9 0.9 %copy-start = (bf16[128,384]{1,0:T(8,128)(2,1)S(1)}, bf16[128,384]{1,0:T(8,128)(2,1)}, u32[]{:S(2)}) copy-start(bf16[128,384]{1,0:T(8,128)(2,1)} %get-tuple-element.13) | copy-start | bytes 294916

commit v5 on v4

--- a/solution.py
+++ b/solution.py
@@ -456,9 +456,8 @@
         after(1, (send_two_hops, 3))
         after(3, (send_two_hops, 2), (reduce_near, 3))
         after(5, (reduce_near, 2), (reduce_far, 3))
-        after(6, (send_two_hops, 1))
+        after(6, (send_one_hop, 1))
         after(7, (reduce_far, 2))
-        after(8, (reduce_near, 1))
         return 0
 
     lax.fori_loop(0, 6, gradients, 0)
@@ -482,7 +481,7 @@
     lax.fori_loop(0, 3, late_queries, 0)
     send_one_hop(0)
     late_queries(3, 0)
-    reduce_far(1)
+    reduce_far(1, one_hop=True)
     reduce_far(0, one_hop=True)
 
     dq_in[pl.ds(mine * 4, 4)] = dq_src[mine]
@@ -501,7 +500,8 @@
     lax.fori_loop(0, 8, flip_back, 0)
     outgoing = [pltpu.make_async_copy(q_in, dq_hbm, s_out.at[0])]
     outgoing[0].start()
-    sum_along_z(0, cross, cross, 1).wait_send()
+    for px in (0, 1):
+        sum_along_z(px, cross, cross, 1).wait_send()
     over_x(lambda px: total_move(px, px).wait_recv())
     for g in range(GROUPS):
         kt[g * WIDTH : (g + 1) * WIDTH, :] = fin[g, 0:96, :]

time: 78.7 us -> 78.6 us (level)
  no operation moved by 1% of the time
where the time goes in v5:
time: 78.6 us; the launch traced here: 78.4 us
  Pallas kernels  71.2 us (91%)
  local copies, waits for them, and re-layouts  4.31 us (5%)
  other arithmetic  1.54 us (2%)
  between operations  1.34 us (2%)
    pallas_call x1, Pallas kernels, per_device(): pl.pallas_call(kernel, out_shape=(shape((128, 3072), BF16), shape((128, 3...  71.2 us
    unnamed x11, local copies, waits for them, and re-layouts  4.31 us

profile of v5, /device:TPU:1, one launch (start us, length us, event | category | flops | bytes accessed | tf_op | source)
XLA Modules:
  0.0 78.4 jit_solution(9520362932957443051)
XLA Ops:
  1.3 0.0 copy-start.2
  1.3 0.6 copy-done.2
  1.9 0.2 convert_reduce_fusion
  2.1 0.0 copy-start.3
  2.1 0.6 select_reduce_fusion.perm
  2.7 0.0 copy-done.3
  2.7 0.1 multiply_cosine_fusion
  2.9 0.6 pad_maximum_fusion.turn
  3.5 71.2 %shard_map.94 = (bf16[128,3072]{1,0:T(8,128)(2,1)}, bf16[128,384]{1,0:T(8,128)(2,1)}, bf16[128,384]{1,0:T(8,128)(2,1)}) custom-call(s32[32]{0:T(128)} %select_reduce_fusion.perm, s32[32]{0:T(128)} %copy-done.3, f32[2,24,128]{2,1,0:T(8,128)} %pad_maximum_fusion.turn, bf16[128,3072]{1,0:T(8,128)(2,1)} %q_hbm.1, bf16[128,384]{1,0:T(8,128)(2,1)} %k_hbm.1, ...), custom_call_target="tpu_custom_call" | custom-call | flops 8000000000 | bytes 4000000 | tf_op jit(solution)/shard_map/pallas_call | solution.py:572
  74.7 0.0 copy-start.1
  74.7 2.1 %copy.14 = bf16[128,3072]{1,0:T(8,128)(2,1)} copy(bf16[128,3072]{1,0:T(8,128)(2,1)} %get-tuple-element.11) | data formatting | bytes 1572864
  76.8 0.0 copy-done.1
  76.8 0.0 copy-start
  76.8 0.6 copy.15
  77.5 0.3 copy-done
  77.7 0.6 copy.16
  (4 shorter events, 0.0 us)
Async XLA Ops:
  1.3 0.7 copy-start.2
  2.1 0.6 copy-start.3
  74.7 2.1 %copy-start.1 = (bf16[128,384]{1,0:T(8,128)(2,1)S(1)}, bf16[128,384]{1,0:T(8,128)(2,1)}, u32[]{:S(2)}) copy-start(bf16[128,384]{1,0:T(8,128)(2,1)} %get-tuple-element.12) | copy-start | bytes 294916
  76.8 0.9 %copy-start = (bf16[128,384]{1,0:T(8,128)(2,1)S(1)}, bf16[128,384]{1,0:T(8,128)(2,1)}, u32[]{:S(2)}) copy-start(bf16[128,384]{1,0:T(8,128)(2,1)} %get-tuple-element.13) | copy-start | bytes 294916
